TPU v7x, 128 devices: a whole 4x4x4 slice. The times are simulated.
128 devices in a mesh: head: 16 (over y, z), qblk: 8 (over x, core).
Axes of the slice: x: 4, y: 4, z: 4, core: 2. Of those that a mesh axis runs over, the one named last changes fastest.
Arguments:
- residual: bfloat16 [4096, 2048], P(('qblk', 'head')), may hold values from -6 to 6
- queries: bfloat16 [4096, 4096], P('qblk', 'head'), may hold values from -30 to 30
- key_cache: bfloat16 [4, 2048, 128], P(None, 'qblk'), may hold values from -6 to 6
- value_cache: bfloat16 [4, 2048, 128], P(None, 'qblk'), may hold values from -6 to 6
- visible_len: int32 [4096], P('qblk'), may hold values from 256 to 2048
- out_weight: bfloat16 [4096, 2048], P('head'), may hold values from -0.5 to 0.5
- norm_gain: float32 [2048], replicated, may hold values from 0.1 to 1.9
- expert_ids: int32 [4096, 8], P(('qblk', 'head')), may hold values from 0 to 127, all different within a row; in each aligned block of 32 rows (0 to 31, 32 to 63, ...) at most 4 rows name the same one
- route_weights: float32 [4096, 8], P(('qblk', 'head')), may hold values from 0.02 to 0.3
- w_gate: bfloat16 [128, 2048, 768], P(('head', 'qblk')), may hold values from -0.125 to 0.125
- w_up: bfloat16 [128, 2048, 768], P(('head', 'qblk')), may hold values from -0.125 to 0.125
- w_down: bfloat16 [128, 768, 2048], P(('head', 'qblk')), may hold values from -0.21875 to 0.21875
Outputs:
- layer_out: bfloat16 [4096, 2048], P(('qblk', 'head'))
Inputs may be any that keep to these rules, and one draw needn't show every extreme that they name: `expert_ids`: each row names 8 different experts; in each aligned block of 32 rows (the rows of one device) no expert is named more than 4 times, and some block names some expert exactly 4 times.
All inputs are finite; a program needn't handle non-finite values.
Results may differ from a plain program's by a relative error of at most 0.012.
Values may be sent and summed in bfloat16 or wider, within the bound.
A program may use at most 64 MiB of HBM per device.

v0:
```python
import jax
import jax.numpy as jnp
from jax import lax
from jax.sharding import PartitionSpec as P

D = 2048
QH = 32
KVH = 4
HD = 128


def attend(running, key_block, value_block, query_heads, visible_len):
    run_max, run_sum, numerator = running
    piece_len = key_block.shape[0]
    scores = jnp.einsum(
        "thd,nd->thn", query_heads, key_block, preferred_element_type=jnp.float32
    ) * HD ** (-0.5)
    key_pos = jnp.arange(piece_len, dtype=jnp.int32)
    visible = key_pos[None, None, :] < visible_len[:, None, None]
    scores = jnp.where(visible, scores, -1e30)
    new_max = jnp.maximum(run_max, jnp.max(scores, axis=2))
    exp_scores = jnp.where(visible, jnp.exp(scores - new_max[:, :, None]), 0.0)
    run_sum = jnp.sum(exp_scores, axis=2)
    numerator = jnp.einsum(
        "thn,nd->thd",
        exp_scores.astype(jnp.bfloat16),
        value_block,
        preferred_element_type=jnp.float32,
    )
    return (new_max, run_sum, numerator)


def expert_ffn(arrived, gate_matrix, up_matrix, down_matrix):
    flat_rows = arrived.reshape(-1, arrived.shape[-1])
    gate_act = jnp.dot(flat_rows, gate_matrix, preferred_element_type=jnp.float32)
    up_act = jnp.dot(flat_rows, up_matrix, preferred_element_type=jnp.float32)
    hidden = (jax.nn.silu(gate_act) * up_act).astype(jnp.bfloat16)
    expert_out = jnp.dot(hidden, down_matrix, preferred_element_type=jnp.float32).astype(
        jnp.bfloat16
    )
    return expert_out.reshape(arrived.shape)


def per_device(
    residual,
    queries,
    key_cache,
    value_cache,
    visible_len,
    out_weight,
    norm_gain,
    expert_ids,
    route_weights,
    w_gate,
    w_up,
    w_down,
):
    head_count = lax.axis_size("head")
    qblk_count = lax.axis_size("qblk")
    query_rows = queries.shape[0]
    local_heads = queries.shape[1] // HD
    kv_index = lax.axis_index("head") * local_heads // (QH // KVH)
    query_heads = queries.reshape(query_rows, local_heads, HD)
    start_state = (
        jnp.full((query_rows, local_heads), -1e30, jnp.float32),
        jnp.zeros((query_rows, local_heads), jnp.float32),
        jnp.zeros((query_rows, local_heads, HD), jnp.float32),
    )
    key_block = lax.dynamic_index_in_dim(
        lax.all_gather(key_cache, "qblk", axis=1, tiled=True), kv_index, 0, keepdims=False
    )
    value_block = lax.dynamic_index_in_dim(
        lax.all_gather(value_cache, "qblk", axis=1, tiled=True), kv_index, 0, keepdims=False
    )
    final_state = attend(start_state, key_block, value_block, query_heads, visible_len)
    attended = (
        (final_state[2] / final_state[1][:, :, None])
        .astype(jnp.bfloat16)
        .reshape(query_rows, local_heads * HD)
    )
    projected = lax.psum_scatter(
        jnp.dot(attended, out_weight, preferred_element_type=jnp.float32).astype(jnp.bfloat16),
        "head",
        scatter_dimension=0,
        tiled=True,
    ).astype(jnp.float32)
    hidden_state = residual.astype(jnp.float32) + projected
    mean_square = jnp.mean(hidden_state * hidden_state, axis=1, keepdims=True)
    normed = (hidden_state * lax.rsqrt(mean_square + 1e-06) * norm_gain).astype(jnp.bfloat16)
    token_rows = residual.shape[0]
    top_count = expert_ids.shape[1]
    expert_count = head_count * qblk_count
    capacity = 2 * token_rows * top_count // expert_count
    flat_ids = expert_ids.reshape(token_rows * top_count)
    onehot = (flat_ids[:, None] == jnp.arange(expert_count, dtype=jnp.int32)[None, :]).astype(
        jnp.int32
    )
    running_rank = jnp.cumsum(onehot, axis=0) - 1
    slot_pos = jnp.sum(onehot * running_rank, axis=1)
    slot_index = flat_ids * capacity + slot_pos
    repeated = jnp.repeat(normed, top_count, axis=0)
    outgoing = jnp.zeros((expert_count * capacity, D), jnp.bfloat16).at[slot_index].set(repeated)
    outgoing = outgoing.reshape(expert_count, capacity, D)
    expert_out = expert_ffn(
        lax.all_to_all(outgoing, ("head", "qblk"), split_axis=0, concat_axis=0, tiled=True),
        w_gate[0],
        w_up[0],
        w_down[0],
    )
    returned_rows = lax.all_to_all(
        expert_out, ("head", "qblk"), split_axis=0, concat_axis=0, tiled=True
    )
    picked = returned_rows.reshape(expert_count * capacity, D)[slot_index]
    picked = picked.reshape(token_rows, top_count, D).astype(jnp.float32)
    expert_mix = jnp.sum(route_weights[:, :, None] * picked, axis=1)
    return (hidden_state + expert_mix).astype(jnp.bfloat16)


def solution(mesh):
    in_specs = (
        P(("qblk", "head"), None),
        P("qblk", "head"),
        P(None, "qblk", None),
        P(None, "qblk", None),
        P("qblk"),
        P("head", None),
        P(),
        P(("qblk", "head"), None),
        P(("qblk", "head"), None),
        P(("head", "qblk"), None, None),
        P(("head", "qblk"), None, None),
        P(("head", "qblk"), None, None),
    )
    out_specs = P(("qblk", "head"), None)
    return jax.shard_map(
        per_device, mesh=mesh, in_specs=in_specs, out_specs=out_specs, check_vma=False
    )
```

profile of v0, /device:TPU:1, one launch (start us, length us, event | category | flops | bytes accessed | tf_op | source)
XLA Modules:
  0.0 272.5 jit_solution(2718837661514652599)
XLA Ops:
  6.5 0.7 all-gather.3.cloned.1.call-update
  7.3 0.7 all-gather.5.cloned.1.call-update
  8.1 2.5 iota_compare_fusion
  10.6 27.3 %all-gather.3.cloned.1.call-done = bf16[4,2048,128]{2,1,0:T(8,128)(2,1)} async-done(((bf16[4,256,128]{2,1,0:T(8,128)(2,1)}), bf16[4,2048,128]{2,1,0:T(8,128)(2,1)}) %all-gather.3.cloned.1.call-update) | async-done | bytes 2097168 | tf_op jit(solution)/shard_map/all_gather | solution.py:70
  37.8 3.3 %fusion = (f32[512,2]{0,1:T(2,128)S(1)}, f32[2048,512,2]{1,0,2:T(8,128)S(1)}) fusion(pred[512,2048]{0,1:T(8,128)(4,1)} %iota_compare_fusion, bf16[4,2048,128]{2,1,0:T(8,128)(2,1)} %all-gather.3.cloned.1.call-done, s32[]{:T(128)S(6)} %select_n.29, bf16[512,256]{1,0:T(8,128)(2,1)} %param.13), kind=kOutput, calls=%fused_computation.4 | convolution fusion | flops 543161344 | bytes 10227716 | tf_op jit(solution)/shard_map/thd,nd->thn/dot_general | solution.py:15
  41.2 3.2 %copy-done.1 = f32[2048,512,2]{1,0,2:T(8,128)} copy-done((f32[2048,512,2]{1,0,2:T(8,128)}, f32[2048,512,2]{1,0,2:T(8,128)S(1)}, u32[]{:S(2)}) %copy-start.1) | copy-done | bytes 8388632
  44.4 2.2 fusion.1
  46.7 18.4 %all-gather.5.cloned.1.call-done = bf16[4,2048,128]{2,1,0:T(8,128)(2,1)} async-done(((bf16[4,256,128]{2,1,0:T(8,128)(2,1)}), bf16[4,2048,128]{2,1,0:T(8,128)(2,1)}) %all-gather.5.cloned.1.call-update) | async-done | bytes 2097168 | tf_op jit(solution)/shard_map/all_gather | solution.py:73
  65.0 6.4 %fusion.24 = bf16[512,2,128]{0,2,1:T(8,128)(2,1)S(1)} fusion(f32[2048,512,2]{1,0,2:T(8,128)} %copy-done.1, f32[512,2]{0,1:T(2,128)S(1)} %broadcast_maximum_fusion, pred[512,2048]{0,1:T(8,128)(4,1)} %iota_compare_fusion, bf16[4,2048,128]{2,1,0:T(8,128)(2,1)} %all-gather.5.cloned.1.call-done, s32[]{:T(128)S(6)} %select_n.29, f32[512,2]{0,1:T(2,128)S(1)} %fusion.1), kind=kOutput, calls=%fused_computation.25 | convolution fusion | flops 547618816 | bytes 10231812 | tf_op jit(solution)/shard_map/thn,nd->thd/dot_general | solution.py:24
  71.5 2.1 convolution_convert_fusion
  73.6 0.7 copy-done.6
  74.3 0.1 eq.29
  74.5 0.1 copy.24
  74.6 0.2 fusion.37
  75.1 0.1 mul.72
  75.1 0.2 fusion.38
  75.3 71.3 %reduce-scatter.2.cloned.1.call-done = bf16[32,2048]{1,0:T(8,128)(2,1)} async-done(((bf16[512,2048]{1,0:T(8,128)(2,1)}), bf16[32,2048]{1,0:T(8,128)(2,1)}) %reduce-scatter.2.cloned.1.call-update) | async-done | bytes 131088 | tf_op jit(solution)/shard_map/reduce_scatter | solution.py:81
  146.6 1.1 multiply_reduce_fusion
  147.7 1.0 multiply_convert_fusion.1
  148.7 3.7 %scatter_custom_fusion = bf16[512,2048]{1,0:T(8,128)(2,1)} fusion(s32[256]{0:T(256)S(1)} %bitcast.73, bf16[]{:T(256)} %constant.56.clone.1, bf16[32,2048]{1,0:T(8,128)(2,1)S(1)} %multiply_convert_fusion.1), kind=kCustom, calls=%fused_computation.21 | custom fusion | bytes 2228226 | tf_op jit(solution)/shard_map/scatter | solution.py:102
  152.4 4.1 %reshape.111 = bf16[128,4,2048]{2,1,0:T(4,128)(2,1)} reshape(bf16[512,2048]{1,0:T(8,128)(2,1)} %scatter_custom_fusion) | data formatting | bytes 4194304 | tf_op jit(solution)/shard_map/reshape | solution.py:103
  156.5 39.7 %all_to_all.10 = bf16[128,4,2048]{2,1,0:T(4,128)(2,1)} all-to-all(bf16[128,4,2048]{2,1,0:T(4,128)(2,1)} %reshape.111), channel_id=1, replica_groups=mesh['head'=16,'qblk'=8] {'head','qblk'}, dimensions={0} | all-to-all | bytes 4194304 | tf_op jit(solution)/shard_map/all_to_all | solution.py:105
  196.2 4.0 %reshape.112 = bf16[512,2048]{1,0:T(8,128)(2,1)} reshape(bf16[128,4,2048]{2,1,0:T(4,128)(2,1)} %all_to_all.10) | data formatting | bytes 4194304 | tf_op jit(solution)/shard_map/reshape | solution.py:34
  200.1 5.5 %fusion.10 = f32[512,768]{1,0:T(8,128)} fusion(bf16[512,2048]{1,0:T(8,128)(2,1)} %reshape.112, bf16[1,2048,768]{2,1,0:T(8,128)(2,1)} %param.21), kind=kOutput, calls=%fused_computation.14 | convolution fusion | flops 1610612736 | bytes 6815744 | tf_op jit(solution)/shard_map/dot_general | solution.py:35
  205.6 8.2 %fusion.12 = bf16[512,2048]{1,0:T(8,128)(2,1)} fusion(bf16[1,768,2048]{2,1,0:T(8,128)(2,1)S(1)} %copy-done, f32[512,768]{1,0:T(8,128)} %fusion.10, bf16[512,2048]{1,0:T(8,128)(2,1)} %reshape.112, bf16[1,2048,768]{2,1,0:T(8,128)(2,1)} %param.22), kind=kOutput, calls=%fused_computation.17 | convolution fusion | flops 3224633344 | bytes 12058624 | tf_op jit(solution)/shard_map/dot_general | solution.py:38
  213.8 4.1 %reshape.113 = bf16[128,4,2048]{2,1,0:T(4,128)(2,1)} reshape(bf16[512,2048]{1,0:T(8,128)(2,1)} %fusion.12) | data formatting | bytes 4194304 | tf_op jit(solution)/shard_map/reshape | solution.py:41
  218.0 5.6 %all-to-all-start.1 = ((bf16[128,4,2048]{2,1,0:T(4,128)(2,1)}), bf16[128,4,2048]{2,1,0:T(4,128)(2,1)}, u32[]{:S(2)}, u32[]{:S(2)}) async-start(bf16[128,4,2048]{2,1,0:T(4,128)(2,1)} %reshape.113), calls=%async_computation.2 | async-start | bytes 4194304 | tf_op jit(solution)/shard_map/all_to_all | solution.py:110
  223.6 30.2 %all-to-all-done.1 = bf16[128,4,2048]{2,1,0:T(4,128)(2,1)} async-done(((bf16[128,4,2048]{2,1,0:T(4,128)(2,1)}), bf16[128,4,2048]{2,1,0:T(4,128)(2,1)}, u32[]{:S(2)}, u32[]{:S(2)}) %all-to-all-start.1) | async-done | bytes 2097184 | tf_op jit(solution)/shard_map/all_to_all | solution.py:110
  253.8 4.0 %reshape.114 = bf16[512,2048]{1,0:T(8,128)(2,1)} reshape(bf16[128,4,2048]{2,1,0:T(4,128)(2,1)} %all-to-all-done.1) | data formatting | bytes 4194304 | tf_op jit(solution)/shard_map/reshape | solution.py:113
  257.8 5.2 %gather_fusion = bf16[256,2048]{1,0:T(8,128)(2,1)} fusion(bf16[512,2048]{1,0:T(8,128)(2,1)} %reshape.114, s32[1024]{0:T(1024)S(1)} %pad_clamp_fusion), kind=kCustom, calls=%fused_computation | custom fusion | bytes 2098176 | tf_op jit(solution)/shard_map/gather | solution.py:113
  263.1 2.2 fusion.15
  265.3 0.7 add_convert_fusion
  (34 shorter events, 0.6 us)
Async XLA Ops:
  6.5 199.1 %copy-start = (bf16[1,768,2048]{2,1,0:T(8,128)(2,1)S(1)}, bf16[1,768,2048]{2,1,0:T(8,128)(2,1)}, u32[]{:S(2)}) copy-start(bf16[1,768,2048]{2,1,0:T(8,128)(2,1)} %param.23) | copy-start | bytes 9437188
  6.5 31.3 %all-gather.3.cloned.1.call-start = ((), (), s32[]{:S(2)}) async-start(), calls=%async_computation.3 | async-start | bytes 2359296 | tf_op jit(solution)/shard_map/all_gather | solution.py:70
  7.3 57.8 %all-gather.5.cloned.1.call-start = ((), (), s32[]{:S(2)}) async-start(), calls=%async_computation.4 | async-start | bytes 2359296 | tf_op jit(solution)/shard_map/all_gather | solution.py:73
  8.0 138.6 %reduce-scatter.2.cloned.1.call-start = ((), (), s32[]{:S(2)}) async-start(), calls=%async_computation.5 | async-start | bytes 2228224 | tf_op jit(solution)/shard_map/reduce_scatter | solution.py:81
  37.8 6.6 %copy-start.2 = (pred[512,2048]{0,1:T(8,128)(4,1)S(1)}, pred[512,2048]{0,1:T(8,128)(4,1)}, u32[]{:S(2)}) copy-start(pred[512,2048]{0,1:T(8,128)(4,1)} %iota_compare_fusion) | copy-start | bytes 3145732
  41.2 3.2 %copy-start.1 = (f32[2048,512,2]{1,0,2:T(8,128)}, f32[2048,512,2]{1,0,2:T(8,128)S(1)}, u32[]{:S(2)}) copy-start(f32[2048,512,2]{1,0,2:T(8,128)S(1)} %get-tuple-element.6) | copy-start | bytes 25165828
  65.0 6.5 %copy-start.5 = (bf16[256,2048]{1,0:T(8,128)(2,1)S(1)}, bf16[256,2048]{1,0:T(8,128)(2,1)}, u32[]{:S(2)}) copy-start(bf16[256,2048]{1,0:T(8,128)(2,1)} %param.17) | copy-start | bytes 3145732
  73.6 0.7 copy-start.6
  73.6 73.0 %copy-start.3 = (bf16[32,2048]{1,0:T(8,128)(2,1)S(1)}, bf16[32,2048]{1,0:T(8,128)(2,1)}, u32[]{:S(2)}) copy-start(bf16[32,2048]{1,0:T(8,128)(2,1)} %param.12) | copy-start | bytes 393220
  73.6 74.1 %copy-start.7 = (f32[2048]{0:T(1024)S(1)}, f32[2048]{0:T(1024)}, u32[]{:S(2)}) copy-start(f32[2048]{0:T(1024)} %param.18) | copy-start | bytes 24580
  218.0 5.6 %copy-start.8 = (f32[32,8]{0,1:T(8,128)S(1)}, f32[32,8]{0,1:T(8,128)}, u32[]{:S(2)}) copy-start(f32[32,8]{0,1:T(8,128)} %param.20) | copy-start | bytes 3076
  218.0 35.9 %all-to-all-start.1 = ((bf16[128,4,2048]{2,1,0:T(4,128)(2,1)}), bf16[128,4,2048]{2,1,0:T(4,128)(2,1)}, u32[]{:S(2)}, u32[]{:S(2)}) async-start(bf16[128,4,2048]{2,1,0:T(4,128)(2,1)} %reshape.113), calls=%async_computation.2 | async-start | bytes 4194304 | tf_op jit(solution)/shard_map/all_to_all | solution.py:110
  257.8 7.5 %copy-start.4 = (bf16[32,2048]{1,0:T(8,128)(2,1)S(1)}, bf16[32,2048]{1,0:T(8,128)(2,1)}, u32[]{:S(2)}) copy-start(bf16[32,2048]{1,0:T(8,128)(2,1)} %reduce-scatter.2.cloned.1.call-done) | copy-start | bytes 393220
Sparse Core Ops, SparseCore 0:
  9.1 28.7 all-gather.2
  39.5 25.4 all-gather.4
  73.7 72.8 reduce-scatter.1
where the time goes:
time: 273 us
  waiting for transfers between devices  149 us (55%)
  blocking collectives  39.7 us (15%)
  local copies, waits for them, and re-layouts  29.6 us (11%)
  matrix products  25.6 us (9%)
  between operations  13.3 us (5%)
  other arithmetic  10.2 us (4%)
  starting transfers between devices  5.64 us (2%)
    reduce_scatter x1, waiting for transfers between devices, per_device(): lax.psum_scatter(jnp.dot(attended, out_weight, preferred_element_type=jnp...  71.3 us
    all_to_all x1, blocking collectives, per_device(): lax.all_to_all(outgoing, ('head', 'qblk'), split_axis=0, concat_axis=0, t...  39.7 us
    all_to_all x1, waiting for transfers between devices, per_device(): lax.all_to_all(expert_out, ('head', 'qblk'), split_axis=0, concat_axis=0,...  30.2 us
    all_gather x1, waiting for transfers between devices, per_device(): lax.all_gather(key_cache, 'qblk', axis=1, tiled=True)  27.3 us
    all_gather x1, waiting for transfers between devices, per_device(): lax.all_gather(value_cache, 'qblk', axis=1, tiled=True)  18.4 us
    dot_general x1, matrix products, expert_ffn(): jnp.dot(hidden, down_matrix, preferred_element_type=jnp.float32)  8.23 us
    dot_general x1, matrix products, attend(): jnp.einsum('thn,nd->thd', exp_scores.astype(jnp.bfloat16), value_block, p...  6.45 us
    all_to_all x1, starting transfers between devices, per_device(): lax.all_to_all(expert_out, ('head', 'qblk'), split_axis=0, concat_axis=0,...  5.56 us
  transfers between devices with their start and end apart: 4, of which 4 were waited for; matrix products, arithmetic and copies ran while one was open for 3% of the time, Pallas kernels for 0%

commit v1 on v0

v1 whole, which is shorter than its diff:
```python
import jax
import jax.numpy as jnp
from jax import lax
from jax.experimental import pallas as pl
from jax.experimental.pallas import tpu as pltpu
from jax.sharding import PartitionSpec as P

MESH = pl.DeviceIdType.MESH
F32, BF16 = jnp.float32, jnp.bfloat16
D = 2048
HD = 128
FF = 768
HALF = D // 2
NEG = -1e30
QSCALE = HD ** (-0.5) * 1.4426950408889634
VMEM_LIMIT = 58 * 1024 * 1024


def dot(a, b):
    return jnp.dot(a, b, preferred_element_type=F32)


def dot_nt(a, b):
    return lax.dot_general(a, b, (((1,), (1,)), ((), ())), preferred_element_type=F32)


def dot_tn(a, b):
    return lax.dot_general(a, b, (((0,), (0,)), ((), ())), preferred_element_type=F32)


def wait_bytes(ref, sem):
    pltpu.make_async_copy(ref, ref, sem).wait()


def attention_kernel(
    q_ref, key_ref, value_ref, vis_ref, res_ref, gain_ref, w_ref,
    hid_ref, normed_ref,
    kv, w_buf, vt, top, den, acc, att, part, got, mid, got2,
    own_sem, w_sem, kv_send, kv_recv, send1, recv1, send2, recv2,
):
    head, qblk = lax.axis_index("head"), lax.axis_index("qblk")
    yy, zz = head // 4, lax.rem(head, 4)
    xx, core = qblk // 2, lax.rem(qblk, 2)
    sibling = 2 * xx + 1 - core

    def remote(src, dst, ssem, rsem, h, q):
        c = pltpu.make_async_remote_copy(
            src_ref=src, dst_ref=dst, send_sem=ssem, recv_sem=rsem,
            device_id=(h, q), device_id_type=MESH,
        )
        c.start()

    w_copy = pltpu.make_async_copy(w_ref, w_buf, w_sem)
    w_copy.start()
    for j, src in enumerate((key_ref, value_ref)):
        remote(src.at[yy], kv.at[qblk, j], kv_send, kv_recv.at[qblk], head, sibling)
        for dx in (1, 3, 2):
            peer = 2 * lax.rem(xx + dx, 4) + core
            remote(src.at[yy], kv.at[qblk, j], kv_send, kv_recv.at[qblk], head, peer)
    for j, src in enumerate((key_ref, value_ref)):
        pltpu.make_async_copy(src.at[yy], kv.at[qblk, j], own_sem).start()
    wait_bytes(kv.at[qblk], own_sem)

    top[...] = jnp.full(top.shape, NEG, F32)
    den[...] = jnp.zeros(den.shape, F32)
    acc[...] = jnp.zeros(acc.shape, F32)

    for dx in (0, 1, 3, 2):
        chip = lax.rem(xx + dx, 4)
        if dx:
            mine = 2 * chip + core
            wait_bytes(kv.at[mine], kv_recv.at[mine])
            remote(kv.at[mine], kv.at[mine], kv_send, kv_recv.at[mine], head, sibling)
        other = 2 * chip + 1 - core
        wait_bytes(kv.at[other], kv_recv.at[other])
        keys = kv[pl.ds(2 * chip, 2), 0].reshape(512, HD)
        vt[...] = kv[pl.ds(2 * chip, 2), 1].reshape(512, HD).astype(F32).T.astype(BF16)
        base = chip * 512

        def rows(i, carry, keys=keys, base=base):
            h, t0 = i // 2, pl.multiple_of(lax.rem(i, 2) * 256, 256)
            q = q_ref[pl.ds(t0, 256), pl.ds(pl.multiple_of(h * HD, HD), HD)]
            cols = pl.ds(pl.multiple_of(i * 256, 256), 256)
            s = dot_nt(keys, q)
            seen = vis_ref[:, pl.ds(t0, 256)] - base
            s = jnp.where(lax.broadcasted_iota(jnp.int32, s.shape, 0) < seen, s, NEG)
            old = top[:, cols]
            new = jnp.maximum(old, jnp.max(s, axis=0, keepdims=True))
            p = jnp.exp2((s - new) * QSCALE)
            scale = jnp.exp2((old - new) * QSCALE)
            top[:, cols] = new
            den[:, cols] = den[:, cols] * scale + jnp.sum(p, axis=0, keepdims=True)
            acc[:, cols] = acc[:, cols] * scale + dot(vt[...], p.astype(BF16))
            return carry

        lax.fori_loop(0, 4, rows, 0)

    for h in range(2):
        cols = slice(h * 512, (h + 1) * 512)
        att[:, h * HD:(h + 1) * HD] = (acc[:, cols] / den[:, cols]).T.astype(BF16)

    w_copy.wait()
    for d in (2, 1, 3, 0):
        z2, y2 = lax.rem(zz + d, 4), lax.rem(yy + d, 4)
        a0 = jnp.concatenate(
            [att[pl.ds(pl.multiple_of((i * 4 + z2) * 32, 32), 32), :] for i in range(4)], axis=0
        )
        part[0, z2] = dot(a0, w_buf[:, :HALF]).astype(BF16)
        if d:
            remote(part.at[0, z2], got.at[0, zz], send1, recv1.at[0, zz], yy * 4 + z2, qblk)
        a1 = att[pl.ds(pl.multiple_of(y2 * 128, 128), 128), :]
        part[1, y2] = dot(a1, w_buf[:, HALF:]).astype(BF16)
        if d:
            remote(part.at[1, y2], got.at[1, yy], send1, recv1.at[1, yy], y2 * 4 + zz, qblk)

    sum0 = part[0, zz].astype(F32)
    sum1 = part[1, yy].astype(F32)
    for d in (1, 3, 2):
        z2, y2 = lax.rem(zz + d, 4), lax.rem(yy + d, 4)
        wait_bytes(got.at[0, z2], recv1.at[0, z2])
        sum0 += got[0, z2].astype(F32)
        wait_bytes(got.at[1, y2], recv1.at[1, y2])
        sum1 += got[1, y2].astype(F32)
    mid[0] = sum0.reshape(4, 32, HALF).astype(BF16)
    mid[1] = sum1.reshape(4, 32, HALF).astype(BF16)
    for d in (2, 1, 3):
        z2, y2 = lax.rem(zz + d, 4), lax.rem(yy + d, 4)
        remote(mid.at[0, y2], got2.at[0, yy], send2, recv2.at[0, yy], y2 * 4 + zz, qblk)
        remote(mid.at[1, z2], got2.at[1, zz], send2, recv2.at[1, zz], yy * 4 + z2, qblk)
    h0 = res_ref[:, :HALF].astype(F32) + mid[0, yy].astype(F32)
    h1 = res_ref[:, HALF:].astype(F32) + mid[1, zz].astype(F32)
    for d in (1, 3, 2):
        z2, y2 = lax.rem(zz + d, 4), lax.rem(yy + d, 4)
        wait_bytes(got2.at[0, y2], recv2.at[0, y2])
        h0 += got2[0, y2].astype(F32)
        wait_bytes(got2.at[1, z2], recv2.at[1, z2])
        h1 += got2[1, z2].astype(F32)
    square = jnp.sum(h0 * h0, axis=1, keepdims=True) + jnp.sum(h1 * h1, axis=1, keepdims=True)
    rs = lax.rsqrt(square * (1.0 / D) + 1e-6)
    hid_ref[:, :HALF] = h0
    hid_ref[:, HALF:] = h1
    normed_ref[:, :HALF] = (h0 * rs * gain_ref[:, :HALF]).astype(BF16)
    normed_ref[:, HALF:] = (h1 * rs * gain_ref[:, HALF:]).astype(BF16)

    wait_bytes(kv.at[pl.ds(0, 7)], kv_send)
    wait_bytes(part.at[:, pl.ds(0, 3)], send1)
    wait_bytes(mid.at[:, pl.ds(0, 3)], send2)


def iota(shape, axis):
    return lax.broadcasted_iota(jnp.int32, shape, axis)


def expert_kernel(
    ids_ref, rw_ref, hid_ref, normed_ref, wg_ref, wu_ref, wd_ref,
    out_ref,
    wg, wu, wd, outbox, inbox, ybox, backbox, mix, x_buf, y_buf,
    w_sem, send1, recv1, send2, recv2,
):
    head, qblk = lax.axis_index("head"), lax.axis_index("qblk")
    me = head * 8 + qblk
    w_copies = [
        pltpu.make_async_copy(src.at[0], dst, w_sem.at[i])
        for i, (src, dst) in enumerate(((wg_ref, wg), (wu_ref, wu), (wd_ref, wd)))
    ]
    for c in w_copies:
        c.start()

    expert = iota((32, 128), 1)
    named = jnp.zeros((32, 128), F32)
    weight = jnp.zeros((32, 128), F32)
    for k in range(8):
        hit = ids_ref[:, k:k + 1] == expert
        named = jnp.where(hit, 1.0, named)
        weight = jnp.where(hit, rw_ref[:, k:k + 1], weight)
    earlier = jnp.where(iota((32, 32), 1) < iota((32, 32), 0), 1.0, 0.0).astype(BF16)
    rank = jnp.where(named > 0.0, dot(earlier, named.astype(BF16)), -1.0)
    rank4 = jnp.concatenate([rank] * 4, axis=0)

    spread = jnp.where(iota((2048, 128), 0) // 16 == iota((2048, 128), 1), 1.0, 0.0).astype(BF16)
    at = dot(spread, rank4.T.astype(BF16))
    j = iota((2048, 128), 0)
    take = (at == lax.rem(j, 4).astype(F32)) & (lax.rem(j // 4, 4) == iota((2048, 128), 1) // 32)
    pick = jnp.where(take, 1.0, 0.0).astype(BF16)
    x4 = jnp.concatenate([normed_ref[:, c * 512:(c + 1) * 512] for c in range(4)], axis=0)
    outbox[...] = dot(pick, x4).astype(BF16)

    def rows16(i):
        return pl.ds(pl.multiple_of(i * 16, 16), 16)

    def dispatch(k, carry):
        e = lax.rem(me + k, 128)
        eh, eq = e // 8, lax.rem(e, 8)
        off = lax.rem(eh - head + 16, 16)
        pltpu.make_async_remote_copy(
            src_ref=outbox.at[rows16(e)], dst_ref=inbox.at[rows16(off * 8 + qblk)],
            send_sem=send1, recv_sem=recv1.at[off // 4],
            device_id=(eh, eq), device_id_type=MESH,
        ).start()
        return carry

    lax.fori_loop(1, 128, dispatch, 0)
    pltpu.make_async_copy(outbox.at[rows16(me)], inbox.at[rows16(qblk)], recv1.at[0]).start()

    spread_t = jnp.where(iota((128, 2048), 1) // 16 == iota((128, 2048), 0), 1.0, 0.0).astype(BF16)
    at_t = dot(rank4.astype(BF16), spread_t)
    jt = iota((128, 2048), 1)
    take_t = (at_t == lax.rem(jt, 4).astype(F32)) & (lax.rem(jt // 4, 4) == iota((128, 2048), 0) // 32)
    high = weight.astype(BF16)
    low = (weight - high.astype(F32)).astype(BF16)
    for i, w in enumerate((high, low)):
        w4 = dot(jnp.concatenate([w] * 4, axis=0), spread_t)
        mix[i] = jnp.where(take_t, w4, 0.0).astype(BF16)

    r, col = iota((128, 128), 0), iota((128, 128), 1)
    source_row = (lax.rem(r, 32) // 4) * 16 + (r // 32) * 4 + lax.rem(r, 4)
    sort = jnp.where(col == source_row, 1.0, 0.0).astype(BF16)
    c_row = (lax.rem(r, 16) // 4) * 32 + (r // 16) * 4 + lax.rem(r, 4)
    unsort = jnp.where(col == c_row, 1.0, 0.0).astype(BF16)

    for c in w_copies:
        c.wait()

    def one_round(rnd, carry):
        block = pl.ds(pl.multiple_of(rnd * 512, 512), 512)
        wait_bytes(inbox.at[block], recv1.at[rnd])
        for i in range(4):
            x = dot(sort, inbox[pl.ds(pl.multiple_of(rnd * 512 + i * 128, 128), 128), :]).astype(BF16)
            for c in range(4):
                x_buf[i * 32:(i + 1) * 32, c * 512:(c + 1) * 512] = x[c * 32:(c + 1) * 32]
        gate = dot(x_buf[...], wg[...])
        up = dot(x_buf[...], wu[...])
        hidden = (gate / (1.0 + jnp.exp(-gate)) * up).astype(BF16)
        y_buf[...] = dot(hidden, wd[...]).astype(BF16)
        for i in range(4):
            y = jnp.concatenate(
                [y_buf[i * 32:(i + 1) * 32, c * 512:(c + 1) * 512] for c in range(4)], axis=0
            )
            ybox[pl.ds(pl.multiple_of(rnd * 512 + i * 128, 128), 128), :] = dot(unsort, y).astype(BF16)

        def send_back(k, carry):
            p = rnd * 32 + k
            sh, sq = lax.rem(head - p // 8 + 16, 16), lax.rem(p, 8)
            remote = sh * 8 + sq != me

            @pl.when(remote)
            def _():
                pltpu.make_async_remote_copy(
                    src_ref=ybox.at[rows16(p)], dst_ref=backbox.at[rows16(me)],
                    send_sem=send2, recv_sem=recv2,
                    device_id=(sh, sq), device_id_type=MESH,
                ).start()

            @pl.when(jnp.logical_not(remote))
            def _():
                pltpu.make_async_copy(ybox.at[rows16(p)], backbox.at[rows16(me)], recv2).start()

            return carry

        lax.fori_loop(0, 32, send_back, 0)
        return carry

    lax.fori_loop(0, 4, one_round, 0)

    wait_bytes(backbox, recv2)
    total = dot(mix[0], backbox[...]) + dot(mix[1], backbox[...])
    for c in range(4):
        f = slice(c * 512, (c + 1) * 512)
        out_ref[:, f] = (hid_ref[:, f] + total[c * 32:(c + 1) * 32]).astype(BF16)
    wait_bytes(outbox.at[pl.ds(0, 127 * 16)], send1)
    wait_bytes(ybox.at[pl.ds(0, 127 * 16)], send2)


def per_device(
    residual, queries, key_cache, value_cache, visible_len, out_weight, norm_gain,
    expert_ids, route_weights, w_gate, w_up, w_down,
):
    vmem, hbm = pl.BlockSpec(memory_space=pltpu.VMEM), pl.BlockSpec(memory_space=pl.ANY)
    dma, scratch = pltpu.SemaphoreType.DMA, pltpu.VMEM
    params = pltpu.CompilerParams(has_side_effects=True, vmem_limit_bytes=VMEM_LIMIT)
    hidden, normed = pl.pallas_call(
        attention_kernel,
        out_shape=(
            jax.ShapeDtypeStruct((32, D), F32),
            jax.ShapeDtypeStruct((32, D), BF16),
        ),
        in_specs=[vmem, hbm, hbm, vmem, vmem, vmem, hbm],
        out_specs=(vmem, vmem),
        scratch_shapes=[
            scratch((8, 2, 256, HD), BF16),
            scratch((256, D), BF16),
            scratch((HD, 512), BF16),
            scratch((1, 1024), F32),
            scratch((1, 1024), F32),
            scratch((HD, 1024), F32),
            scratch((512, 256), BF16),
            scratch((2, 4, 128, HALF), BF16),
            scratch((2, 4, 128, HALF), BF16),
            scratch((2, 4, 32, HALF), BF16),
            scratch((2, 4, 32, HALF), BF16),
            dma, dma, dma, dma((8,)), dma, dma((2, 4)), dma, dma((2, 4)),
        ],
        compiler_params=params,
        name="attention",
    )(
        queries, key_cache, value_cache, visible_len.reshape(1, -1), residual,
        norm_gain.reshape(1, -1), out_weight,
    )
    return pl.pallas_call(
        expert_kernel,
        out_shape=jax.ShapeDtypeStruct((32, D), BF16),
        in_specs=[vmem, vmem, vmem, vmem, hbm, hbm, hbm],
        out_specs=vmem,
        scratch_shapes=[
            scratch((D, FF), BF16),
            scratch((D, FF), BF16),
            scratch((FF, D), BF16),
            scratch((2048, 512), BF16),
            scratch((2048, 512), BF16),
            scratch((2048, 512), BF16),
            scratch((2048, 512), BF16),
            scratch((2, 128, 2048), BF16),
            scratch((128, D), BF16),
            scratch((128, D), BF16),
            dma((3,)), dma, dma((4,)), dma, dma,
        ],
        compiler_params=params,
        name="experts",
    )(expert_ids, route_weights, hidden, normed, w_gate, w_up, w_down)


def solution(mesh):
    in_specs = (
        P(("qblk", "head"), None),
        P("qblk", "head"),
        P(None, "qblk", None),
        P(None, "qblk", None),
        P("qblk"),
        P("head", None),
        P(),
        P(("qblk", "head"), None),
        P(("qblk", "head"), None),
        P(("head", "qblk"), None, None),
        P(("head", "qblk"), None, None),
        P(("head", "qblk"), None, None),
    )
    return jax.shard_map(
        per_device, mesh=mesh, in_specs=in_specs, out_specs=P(("qblk", "head"), None),
        check_vma=False,
    )
```

time: 273 us -> 136 us (0.50)
  waiting for transfers between devices: 149 us -> 0 us
  Pallas kernels: 0 us -> 131 us
  blocking collectives: 39.7 us -> 0 us
  matrix products: 25.6 us -> 0 us
  local copies, waits for them, and re-layouts: 29.6 us -> 4.3 us
  between operations: 13.3 us -> 0.02 us
  other arithmetic: 10.2 us -> 0 us
  starting transfers between devices: 5.64 us -> 0 us
    pallas_call x0 -> x2, Pallas kernels: none -> 131 us  [the longest x1 78.3 us: per_device(): pl.pallas_call(expert_kernel, out_shape=jax.ShapeDtypeStruct((32, D), BF1...]
    reduce_scatter x1 -> x0, waiting for transfers between devices: 71.3 us -> none  [per_device(): lax.psum_scatter(jnp.dot(attended, out_weight, preferred_element_type=jnp...]
    all_gather x2 -> x0, waiting for transfers between devices: 45.6 us -> none  [the longest x1 27.3 us: per_device(): lax.all_gather(key_cache, 'qblk', axis=1, tiled=True)]
    all_to_all x1 -> x0, blocking collectives: 39.7 us -> none  [per_device(): lax.all_to_all(outgoing, ('head', 'qblk'), split_axis=0, concat_axis=0, t...]
    all_to_all x1 -> x0, waiting for transfers between devices: 30.2 us -> none  [per_device(): lax.all_to_all(expert_out, ('head', 'qblk'), split_axis=0, concat_axis=0,...]
    dot_general x5 -> x0, matrix products: 25.6 us -> none  [the longest x1 8.23 us: expert_ffn(): jnp.dot(hidden, down_matrix, preferred_element_type=jnp.float32)]
    reshape x4 -> x0, local copies, waits for them, and re-layouts: 16.1 us -> none  [the longest x1 4.11 us: expert_ffn(): return expert_out.reshape(arrived.shape)]
    reduce_sum x4 -> x0, other arithmetic: 5.68 us -> none  [the longest x1 2.24 us: attend(): run_sum = jnp.sum(exp_scores, axis=2)]
  transfers between devices with their start and end apart: 4 -> 0, of which waited for: 4 -> 0; matrix products, arithmetic and copies ran while one was open for 3% -> 0% of each run, Pallas kernels for 0% -> 0%
where the time goes in v1:
time: 136 us
  Pallas kernels  131 us (96%)
  local copies, waits for them, and re-layouts  4.3 us (3%)
    pallas_call x1, Pallas kernels, per_device(): pl.pallas_call(expert_kernel, out_shape=jax.ShapeDtypeStruct((32, D), BF1...  78.3 us
    pallas_call x1, Pallas kernels, per_device(): pl.pallas_call(attention_kernel, out_shape=(jax.ShapeDtypeStruct((32, D),...  52.9 us
    unnamed x3, local copies, waits for them, and re-layouts  4.3 us

profile of v1, /device:TPU:1, one launch (start us, length us, event | category | flops | bytes accessed | tf_op | source)
XLA Modules:
  0.0 135.5 jit_solution(3023196834033472252)
XLA Ops:
  0.0 1.4 %copy.13.ids_ref = s32[32,8]{1,0:T(8,128)} copy(s32[32,8]{0,1:T(8,128)} %param.19) | data formatting | bytes 2048 | tf_op args[7]
  1.4 1.4 %copy.14.rw_ref = f32[32,8]{1,0:T(8,128)} copy(f32[32,8]{0,1:T(8,128)} %param.20) | data formatting | bytes 2048 | tf_op args[8]
  2.7 52.9 %attention.1 = (f32[32,2048]{1,0:T(8,128)}, bf16[32,2048]{1,0:T(8,128)(2,1)}) custom-call(bf16[512,256]{1,0:T(8,128)(2,1)} %q_ref.1, bf16[4,256,128]{2,1,0:T(8,128)(2,1)} %key_ref.1, bf16[4,256,128]{2,1,0:T(8,128)(2,1)} %value_ref.1, s32[1,512]{1,0:T(1,128)} %bitcast.3, bf16[32,2048]{1,0:T(8,128)(2,1)} %res_ref.1, f32[1,2048]{1,0:T(1,128)} %bitcast.2, ...), custom_call_target="tpu_custom_call" | custom-call | tf_op jit(solution)/shard_map/attention/pallas_call | solution.py:281
  55.6 78.3 %experts.1 = bf16[32,2048]{1,0:T(8,128)(2,1)} custom-call(s32[32,8]{1,0:T(8,128)} %copy.13.ids_ref, f32[32,8]{1,0:T(8,128)} %copy.14.rw_ref, f32[32,2048]{1,0:T(8,128)} %get-tuple-element.7.hid_ref, bf16[32,2048]{1,0:T(8,128)(2,1)} %get-tuple-element.8.normed_ref, bf16[1,2048,768]{2,1,0:T(8,128)(2,1)} %wg_ref.1, bf16[1,2048,768]{2,1,0:T(8,128)(2,1)} %wu_ref.1, ...), custom_call_target="tpu_custom_call" | custom-call | tf_op jit(solution)/shard_map/experts/pallas_call | solution.py:309
  133.9 1.6 %copy.16 = bf16[32,2048]{1,0:T(8,128)(2,1)} copy(bf16[32,2048]{1,0:T(8,128)(2,1)} %experts.1) | data formatting | bytes 262144

commit v2 on v1

--- a/solution.py
+++ b/solution.py
@@ -12,6 +12,7 @@
 FF = 768
 HALF = D // 2
 NEG = -1e30
+STRIDE = 37
 QSCALE = HD ** (-0.5) * 1.4426950408889634
 VMEM_LIMIT = 58 * 1024 * 1024
 
@@ -32,16 +33,57 @@
     pltpu.make_async_copy(ref, ref, sem).wait()
 
 
-def attention_kernel(
-    q_ref, key_ref, value_ref, vis_ref, res_ref, gain_ref, w_ref,
-    hid_ref, normed_ref,
+def iota(shape, axis):
+    return lax.broadcasted_iota(jnp.int32, shape, axis)
+
+
+def rows16(i):
+    return pl.ds(pl.multiple_of(i * 16, 16), 16)
+
+
+def route(ids_ref, rw_ref, pick, mix):
+    expert = iota((128, 32), 0)
+    named = jnp.zeros((128, 32), F32)
+    weight = jnp.zeros((128, 32), F32)
+    for k in range(8):
+        hit = ids_ref[k:k + 1, :] == expert
+        named = jnp.where(hit, 1.0, named)
+        weight = jnp.where(hit, rw_ref[k:k + 1, :], weight)
+    later = jnp.where(iota((32, 32), 0) < iota((32, 32), 1), 1.0, 0.0).astype(BF16)
+    rank = jnp.where(named > 0.0, dot(named.astype(BF16), later), -1.0)
+    four = jnp.where(iota((32, 128), 0) == lax.rem(iota((32, 128), 1), 32), 1.0, 0.0).astype(BF16)
+    rank4 = dot(rank.astype(BF16), four)
+    high = weight.astype(BF16)
+    low = (weight - high.astype(F32)).astype(BF16)
+
+    spread = jnp.where(iota((2048, 128), 0) // 16 == iota((2048, 128), 1), 1.0, 0.0).astype(BF16)
+    at = dot(spread, rank4.astype(BF16))
+    j = iota((2048, 128), 0)
+    take = (at == lax.rem(j, 4).astype(F32)) & (lax.rem(j // 4, 4) == iota((2048, 128), 1) // 32)
+    pick[...] = jnp.where(take, 1.0, 0.0).astype(BF16)
+
+    spread_t = jnp.where(iota((128, 2048), 1) // 16 == iota((128, 2048), 0), 1.0, 0.0).astype(BF16)
+    at_t = dot(rank4.T.astype(BF16), spread_t)
+    jt = iota((128, 2048), 1)
+    take_t = (at_t == lax.rem(jt, 4).astype(F32)) & (lax.rem(jt // 4, 4) == iota((128, 2048), 0) // 32)
+    for i, w in enumerate((high, low)):
+        w4 = dot(dot(w, four).T.astype(BF16), spread_t)
+        mix[i] = jnp.where(take_t, w4, 0.0).astype(BF16)
+
+
+def layer_kernel(
+    q_ref, key_ref, value_ref, vis_ref, res_ref, gain_ref, ids_ref, rw_ref, w_ref, wg_ref, wu_ref, wd_ref,
+    out_ref,
     kv, w_buf, vt, top, den, acc, att, part, got, mid, got2,
     own_sem, w_sem, kv_send, kv_recv, send1, recv1, send2, recv2,
+    wg, wu, wd, hid, x4, pick, outbox, inbox, ybox, backbox, mix, x_buf, y_buf,
+    e_sem, send3, recv3, send4, recv4, plane_sem, all_sem,
 ):
     head, qblk = lax.axis_index("head"), lax.axis_index("qblk")
     yy, zz = head // 4, lax.rem(head, 4)
     xx, core = qblk // 2, lax.rem(qblk, 2)
     sibling = 2 * xx + 1 - core
+    me = head * 8 + qblk
 
     def remote(src, dst, ssem, rsem, h, q):
         c = pltpu.make_async_remote_copy(
@@ -50,8 +92,18 @@
         )
         c.start()
 
-    w_copy = pltpu.make_async_copy(w_ref, w_buf, w_sem)
-    w_copy.start()
+    def signal(sem, h, q):
+        pl.semaphore_signal(sem, inc=1, device_id=(h, q), device_id_type=MESH)
+
+    y_line = [(lax.rem(yy + d, 4) * 4 + zz, qblk) for d in (1, 3, 2)]
+    z_line = [(yy * 4 + lax.rem(zz + d, 4), qblk) for d in (1, 3, 2)]
+    x_line = [(head, lax.rem(qblk + d, 8)) for d in range(1, 8)]
+
+    barrier = pltpu.get_barrier_semaphore()
+    for h, q in x_line + y_line + z_line:
+        signal(barrier, h, q)
+    pl.semaphore_wait(barrier, 13)
+
     for j, src in enumerate((key_ref, value_ref)):
         remote(src.at[yy], kv.at[qblk, j], kv_send, kv_recv.at[qblk], head, sibling)
         for dx in (1, 3, 2):
@@ -59,6 +111,20 @@
             remote(src.at[yy], kv.at[qblk, j], kv_send, kv_recv.at[qblk], head, peer)
     for j, src in enumerate((key_ref, value_ref)):
         pltpu.make_async_copy(src.at[yy], kv.at[qblk, j], own_sem).start()
+    for h, q in y_line:
+        signal(plane_sem, h, q)
+    w_copy = pltpu.make_async_copy(w_ref, w_buf, w_sem)
+    w_copy.start()
+    w_copies = [
+        pltpu.make_async_copy(src.at[0], dst, e_sem.at[i])
+        for i, (src, dst) in enumerate(((wg_ref, wg), (wu_ref, wu), (wd_ref, wd)))
+    ]
+    for c in w_copies:
+        c.start()
+    route(ids_ref, rw_ref, pick, mix)
+    pl.semaphore_wait(plane_sem, 3)
+    for h, q in z_line:
+        signal(all_sem, h, q)
     wait_bytes(kv.at[qblk], own_sem)
 
     top[...] = jnp.full(top.shape, NEG, F32)
@@ -137,80 +203,36 @@
         h1 += got2[1, z2].astype(F32)
     square = jnp.sum(h0 * h0, axis=1, keepdims=True) + jnp.sum(h1 * h1, axis=1, keepdims=True)
     rs = lax.rsqrt(square * (1.0 / D) + 1e-6)
-    hid_ref[:, :HALF] = h0
-    hid_ref[:, HALF:] = h1
-    normed_ref[:, :HALF] = (h0 * rs * gain_ref[:, :HALF]).astype(BF16)
-    normed_ref[:, HALF:] = (h1 * rs * gain_ref[:, HALF:]).astype(BF16)
-
-    wait_bytes(kv.at[pl.ds(0, 7)], kv_send)
-    wait_bytes(part.at[:, pl.ds(0, 3)], send1)
-    wait_bytes(mid.at[:, pl.ds(0, 3)], send2)
-
-
-def iota(shape, axis):
-    return lax.broadcasted_iota(jnp.int32, shape, axis)
-
-
-def expert_kernel(
-    ids_ref, rw_ref, hid_ref, normed_ref, wg_ref, wu_ref, wd_ref,
-    out_ref,
-    wg, wu, wd, outbox, inbox, ybox, backbox, mix, x_buf, y_buf,
-    w_sem, send1, recv1, send2, recv2,
-):
-    head, qblk = lax.axis_index("head"), lax.axis_index("qblk")
-    me = head * 8 + qblk
-    w_copies = [
-        pltpu.make_async_copy(src.at[0], dst, w_sem.at[i])
-        for i, (src, dst) in enumerate(((wg_ref, wg), (wu_ref, wu), (wd_ref, wd)))
-    ]
-    for c in w_copies:
-        c.start()
-
-    expert = iota((32, 128), 1)
-    named = jnp.zeros((32, 128), F32)
-    weight = jnp.zeros((32, 128), F32)
-    for k in range(8):
-        hit = ids_ref[:, k:k + 1] == expert
-        named = jnp.where(hit, 1.0, named)
-        weight = jnp.where(hit, rw_ref[:, k:k + 1], weight)
-    earlier = jnp.where(iota((32, 32), 1) < iota((32, 32), 0), 1.0, 0.0).astype(BF16)
-    rank = jnp.where(named > 0.0, dot(earlier, named.astype(BF16)), -1.0)
-    rank4 = jnp.concatenate([rank] * 4, axis=0)
-
-    spread = jnp.where(iota((2048, 128), 0) // 16 == iota((2048, 128), 1), 1.0, 0.0).astype(BF16)
-    at = dot(spread, rank4.T.astype(BF16))
-    j = iota((2048, 128), 0)
-    take = (at == lax.rem(j, 4).astype(F32)) & (lax.rem(j // 4, 4) == iota((2048, 128), 1) // 32)
-    pick = jnp.where(take, 1.0, 0.0).astype(BF16)
-    x4 = jnp.concatenate([normed_ref[:, c * 512:(c + 1) * 512] for c in range(4)], axis=0)
-    outbox[...] = dot(pick, x4).astype(BF16)
-
-    def rows16(i):
-        return pl.ds(pl.multiple_of(i * 16, 16), 16)
+    hid[:, :HALF] = h0
+    hid[:, HALF:] = h1
+    n0 = (h0 * rs * gain_ref[:, :HALF]).astype(BF16)
+    n1 = (h1 * rs * gain_ref[:, HALF:]).astype(BF16)
+    for c, n in enumerate((n0, n1)):
+        for half in range(2):
+            x4[(2 * c + half) * 32:(2 * c + half + 1) * 32, :] = n[:, half * 512:(half + 1) * 512]
+    pl.semaphore_wait(all_sem, 3)
+
+    outbox[...] = dot(pick[...], x4[...]).astype(BF16)
+
+
+    def partner(k, sign):
+        d = lax.rem(k * STRIDE, 128)
+        py = lax.rem(head // 4 + sign * (d // 32) + 4, 4)
+        pz = lax.rem(lax.rem(head, 4) + sign * lax.rem(d // 8, 4) + 4, 4)
+        px = lax.rem(qblk // 2 + sign * lax.rem(d // 2, 4) + 4, 4)
+        return py * 4 + pz, px * 2 + lax.rem(lax.rem(qblk, 2) + lax.rem(d, 2), 2)
 
     def dispatch(k, carry):
-        e = lax.rem(me + k, 128)
-        eh, eq = e // 8, lax.rem(e, 8)
-        off = lax.rem(eh - head + 16, 16)
+        eh, eq = partner(k, 1)
         pltpu.make_async_remote_copy(
-            src_ref=outbox.at[rows16(e)], dst_ref=inbox.at[rows16(off * 8 + qblk)],
-            send_sem=send1, recv_sem=recv1.at[off // 4],
+            src_ref=outbox.at[rows16(eh * 8 + eq)], dst_ref=inbox.at[rows16(k)],
+            send_sem=send3, recv_sem=recv3.at[k // 32],
             device_id=(eh, eq), device_id_type=MESH,
         ).start()
         return carry
 
     lax.fori_loop(1, 128, dispatch, 0)
-    pltpu.make_async_copy(outbox.at[rows16(me)], inbox.at[rows16(qblk)], recv1.at[0]).start()
-
-    spread_t = jnp.where(iota((128, 2048), 1) // 16 == iota((128, 2048), 0), 1.0, 0.0).astype(BF16)
-    at_t = dot(rank4.astype(BF16), spread_t)
-    jt = iota((128, 2048), 1)
-    take_t = (at_t == lax.rem(jt, 4).astype(F32)) & (lax.rem(jt // 4, 4) == iota((128, 2048), 0) // 32)
-    high = weight.astype(BF16)
-    low = (weight - high.astype(F32)).astype(BF16)
-    for i, w in enumerate((high, low)):
-        w4 = dot(jnp.concatenate([w] * 4, axis=0), spread_t)
-        mix[i] = jnp.where(take_t, w4, 0.0).astype(BF16)
+    pltpu.make_async_copy(outbox.at[rows16(me)], inbox.at[rows16(0)], recv3.at[0]).start()
 
     r, col = iota((128, 128), 0), iota((128, 128), 1)
     source_row = (lax.rem(r, 32) // 4) * 16 + (r // 32) * 4 + lax.rem(r, 4)
@@ -223,7 +245,7 @@
 
     def one_round(rnd, carry):
         block = pl.ds(pl.multiple_of(rnd * 512, 512), 512)
-        wait_bytes(inbox.at[block], recv1.at[rnd])
+        wait_bytes(inbox.at[block], recv3.at[rnd])
         for i in range(4):
             x = dot(sort, inbox[pl.ds(pl.multiple_of(rnd * 512 + i * 128, 128), 128), :]).astype(BF16)
             for c in range(4):
@@ -240,20 +262,20 @@
 
         def send_back(k, carry):
             p = rnd * 32 + k
-            sh, sq = lax.rem(head - p // 8 + 16, 16), lax.rem(p, 8)
-            remote = sh * 8 + sq != me
+            sh, sq = partner(p, -1)
+            remote = p != 0
 
             @pl.when(remote)
             def _():
                 pltpu.make_async_remote_copy(
                     src_ref=ybox.at[rows16(p)], dst_ref=backbox.at[rows16(me)],
-                    send_sem=send2, recv_sem=recv2,
+                    send_sem=send4, recv_sem=recv4,
                     device_id=(sh, sq), device_id_type=MESH,
                 ).start()
 
             @pl.when(jnp.logical_not(remote))
             def _():
-                pltpu.make_async_copy(ybox.at[rows16(p)], backbox.at[rows16(me)], recv2).start()
+                pltpu.make_async_copy(ybox.at[rows16(p)], backbox.at[rows16(me)], recv4).start()
 
             return carry
 
@@ -262,13 +284,16 @@
 
     lax.fori_loop(0, 4, one_round, 0)
 
-    wait_bytes(backbox, recv2)
+    wait_bytes(backbox, recv4)
     total = dot(mix[0], backbox[...]) + dot(mix[1], backbox[...])
     for c in range(4):
         f = slice(c * 512, (c + 1) * 512)
-        out_ref[:, f] = (hid_ref[:, f] + total[c * 32:(c + 1) * 32]).astype(BF16)
-    wait_bytes(outbox.at[pl.ds(0, 127 * 16)], send1)
-    wait_bytes(ybox.at[pl.ds(0, 127 * 16)], send2)
+        out_ref[:, f] = (hid[:, f] + total[c * 32:(c + 1) * 32]).astype(BF16)
+    wait_bytes(kv.at[pl.ds(0, 7)], kv_send)
+    wait_bytes(part.at[:, pl.ds(0, 3)], send1)
+    wait_bytes(mid.at[:, pl.ds(0, 3)], send2)
+    wait_bytes(outbox.at[pl.ds(0, 127 * 16)], send3)
+    wait_bytes(ybox.at[pl.ds(0, 127 * 16)], send4)
 
 
 def per_device(
@@ -277,15 +302,11 @@
 ):
     vmem, hbm = pl.BlockSpec(memory_space=pltpu.VMEM), pl.BlockSpec(memory_space=pl.ANY)
     dma, scratch = pltpu.SemaphoreType.DMA, pltpu.VMEM
-    params = pltpu.CompilerParams(has_side_effects=True, vmem_limit_bytes=VMEM_LIMIT)
-    hidden, normed = pl.pallas_call(
-        attention_kernel,
-        out_shape=(
-            jax.ShapeDtypeStruct((32, D), F32),
-            jax.ShapeDtypeStruct((32, D), BF16),
-        ),
-        in_specs=[vmem, hbm, hbm, vmem, vmem, vmem, hbm],
-        out_specs=(vmem, vmem),
+    return pl.pallas_call(
+        layer_kernel,
+        out_shape=jax.ShapeDtypeStruct((32, D), BF16),
+        in_specs=[vmem, hbm, hbm, vmem, vmem, vmem, vmem, vmem, hbm, hbm, hbm, hbm],
+        out_specs=vmem,
         scratch_shapes=[
             scratch((8, 2, 256, HD), BF16),
             scratch((256, D), BF16),
@@ -299,22 +320,12 @@
             scratch((2, 4, 32, HALF), BF16),
             scratch((2, 4, 32, HALF), BF16),
             dma, dma, dma, dma((8,)), dma, dma((2, 4)), dma, dma((2, 4)),
-        ],
-        compiler_params=params,
-        name="attention",
-    )(
-        queries, key_cache, value_cache, visible_len.reshape(1, -1), residual,
-        norm_gain.reshape(1, -1), out_weight,
-    )
-    return pl.pallas_call(
-        expert_kernel,
-        out_shape=jax.ShapeDtypeStruct((32, D), BF16),
-        in_specs=[vmem, vmem, vmem, vmem, hbm, hbm, hbm],
-        out_specs=vmem,
-        scratch_shapes=[
             scratch((D, FF), BF16),
             scratch((D, FF), BF16),
             scratch((FF, D), BF16),
+            scratch((32, D), F32),
+            scratch((128, 512), BF16),
+            scratch((2048, 128), BF16),
             scratch((2048, 512), BF16),
             scratch((2048, 512), BF16),
             scratch((2048, 512), BF16),
@@ -323,10 +334,16 @@
             scratch((128, D), BF16),
             scratch((128, D), BF16),
             dma((3,)), dma, dma((4,)), dma, dma,
+            pltpu.SemaphoreType.REGULAR, pltpu.SemaphoreType.REGULAR,
         ],
-        compiler_params=params,
-        name="experts",
-    )(expert_ids, route_weights, hidden, normed, w_gate, w_up, w_down)
+        compiler_params=pltpu.CompilerParams(
+            collective_id=0, has_side_effects=True, vmem_limit_bytes=VMEM_LIMIT
+        ),
+        name="layer",
+    )(
+        queries, key_cache, value_cache, visible_len.reshape(1, -1), residual,
+        norm_gain.reshape(1, -1), expert_ids.T, route_weights.T, out_weight, w_gate, w_up, w_down,
+    )
 
 
 def solution(mesh):

time: 136 us -> 98.3 us (0.72)
  Pallas kernels: 131 us -> 96.6 us
  local copies, waits for them, and re-layouts: 4.3 us -> 1.57 us
    pallas_call x2 -> x1, Pallas kernels: 131 us -> 96.6 us  [per_device(): pl.pallas_call(layer_kernel, out_shape=jax.ShapeDtypeStruct((32, D), BF16...]
    unnamed x3 -> x1, local copies, waits for them, and re-layouts: 4.3 us -> 1.57 us
where the time goes in v2:
time: 98.3 us; the launch traced here: 98.1 us
  Pallas kernels  96.6 us (98%)
  local copies, waits for them, and re-layouts  1.57 us (2%)
    pallas_call x1, Pallas kernels, per_device(): pl.pallas_call(layer_kernel, out_shape=jax.ShapeDtypeStruct((32, D), BF16...  96.6 us

profile of v2, /device:TPU:1, one launch (start us, length us, event | category | flops | bytes accessed | tf_op | source)
XLA Modules:
  0.0 98.1 jit_solution(2053587421428360885)
XLA Ops:
  0.0 96.6 %layer.1 = bf16[32,2048]{1,0:T(8,128)(2,1)} custom-call(bf16[512,256]{1,0:T(8,128)(2,1)} %q_ref.1, bf16[4,256,128]{2,1,0:T(8,128)(2,1)} %key_ref.1, bf16[4,256,128]{2,1,0:T(8,128)(2,1)} %value_ref.1, s32[1,512]{1,0:T(1,128)} %bitcast.7, bf16[32,2048]{1,0:T(8,128)(2,1)} %res_ref.1, f32[1,2048]{1,0:T(1,128)} %bitcast.4, s32[8,32]{1,0:T(8,128)} %bitcast.5, ...), custom_call_target="tpu_custom_call" | custom-call | tf_op jit(solution)/shard_map/layer/pallas_call | solution.py:305
  96.6 1.6 %copy.14 = bf16[32,2048]{1,0:T(8,128)(2,1)} copy(bf16[32,2048]{1,0:T(8,128)(2,1)} %layer.1) | data formatting | bytes 262144

commit v3 on v2

--- a/solution.py
+++ b/solution.py
@@ -10,7 +10,6 @@
 D = 2048
 HD = 128
 FF = 768
-HALF = D // 2
 NEG = -1e30
 STRIDE = 37
 QSCALE = HD ** (-0.5) * 1.4426950408889634
@@ -74,8 +73,8 @@
 def layer_kernel(
     q_ref, key_ref, value_ref, vis_ref, res_ref, gain_ref, ids_ref, rw_ref, w_ref, wg_ref, wu_ref, wd_ref,
     out_ref,
-    kv, w_buf, vt, top, den, acc, att, part, got, mid, got2,
-    own_sem, w_sem, kv_send, kv_recv, send1, recv1, send2, recv2,
+    kv, q_buf, w_buf, vt, top, den, acc, att, part, got,
+    own_sem, w_sem, kv_send, kv_recv, q_send, q_recv, w_send, wz_recv, wx_recv, wf_recv, ws_recv, send1, recv1,
     wg, wu, wd, hid, x4, pick, outbox, inbox, ybox, backbox, mix, x_buf, y_buf,
     e_sem, send3, recv3, send4, recv4, plane_sem, all_sem,
 ):
@@ -104,16 +103,32 @@
         signal(barrier, h, q)
     pl.semaphore_wait(barrier, 13)
 
+    for d in (1, 3, 2):
+        z2 = lax.rem(zz + d, 4)
+        remote(q_ref.at[:, z2], q_buf.at[zz], q_send, q_recv.at[zz], yy * 4 + z2, qblk)
     for j, src in enumerate((key_ref, value_ref)):
         remote(src.at[yy], kv.at[qblk, j], kv_send, kv_recv.at[qblk], head, sibling)
         for dx in (1, 3, 2):
             peer = 2 * lax.rem(xx + dx, 4) + core
             remote(src.at[yy], kv.at[qblk, j], kv_send, kv_recv.at[qblk], head, peer)
+    def w_rows(z, first, count):
+        return pl.ds(pl.multiple_of(z * 256 + first, 16), count)
+
+    mine16 = 128 + core * 64 + xx * 16
+    for d in (1, 3, 2):
+        z2 = lax.rem(zz + d, 4)
+        remote(w_ref.at[w_rows(0, mine16, 16)], w_buf.at[w_rows(zz, mine16, 16)],
+               w_send, wx_recv.at[zz], yy * 4 + z2, qblk)
+    for d in (1, 3, 2):
+        z2 = lax.rem(zz + d, 4)
+        remote(w_ref.at[w_rows(0, core * 64, 64)], w_buf.at[w_rows(zz, core * 64, 64)],
+               w_send, wz_recv.at[zz], yy * 4 + z2, qblk)
     for j, src in enumerate((key_ref, value_ref)):
         pltpu.make_async_copy(src.at[yy], kv.at[qblk, j], own_sem).start()
+    pltpu.make_async_copy(q_ref.at[:, zz], q_buf.at[zz], q_recv.at[zz]).start()
     for h, q in y_line:
         signal(plane_sem, h, q)
-    w_copy = pltpu.make_async_copy(w_ref, w_buf, w_sem)
+    w_copy = pltpu.make_async_copy(w_ref, w_buf.at[w_rows(zz, 0, 256)], w_sem)
     w_copy.start()
     w_copies = [
         pltpu.make_async_copy(src.at[0], dst, e_sem.at[i])
@@ -125,7 +140,18 @@
     pl.semaphore_wait(plane_sem, 3)
     for h, q in z_line:
         signal(all_sem, h, q)
+    lane = iota((8, 128), 1)
+    seen_all = jnp.zeros((8, 128), jnp.int32)
+    for i in range(4):
+        block = jnp.broadcast_to(vis_ref[:, i * 128:(i + 1) * 128], (8, 128))
+        block = pltpu.roll(block, lax.rem((i - zz) * 32 + 128, 128), 1)
+        seen_all = jnp.where(lane // 32 == i, block, seen_all)
+    seen_all = jnp.concatenate([seen_all, seen_all], axis=1)[:1]
+
     wait_bytes(kv.at[qblk], own_sem)
+    for d in range(4):
+        z2 = lax.rem(zz + d, 4)
+        wait_bytes(q_buf.at[z2], q_recv.at[z2])
 
     top[...] = jnp.full(top.shape, NEG, F32)
     den[...] = jnp.zeros(den.shape, F32)
@@ -144,12 +170,11 @@
         base = chip * 512
 
         def rows(i, carry, keys=keys, base=base):
-            h, t0 = i // 2, pl.multiple_of(lax.rem(i, 2) * 256, 256)
-            q = q_ref[pl.ds(t0, 256), pl.ds(pl.multiple_of(h * HD, HD), HD)]
+            q = q_buf[i].reshape(128, 2 * HD)
+            q = jnp.concatenate([q[:, :HD], q[:, HD:]], axis=0)
             cols = pl.ds(pl.multiple_of(i * 256, 256), 256)
             s = dot_nt(keys, q)
-            seen = vis_ref[:, pl.ds(t0, 256)] - base
-            s = jnp.where(lax.broadcasted_iota(jnp.int32, s.shape, 0) < seen, s, NEG)
+            s = jnp.where(iota(s.shape, 0) < seen_all - base, s, NEG)
             old = top[:, cols]
             new = jnp.maximum(old, jnp.max(s, axis=0, keepdims=True))
             p = jnp.exp2((s - new) * QSCALE)
@@ -161,55 +186,54 @@
 
         lax.fori_loop(0, 4, rows, 0)
 
-    for h in range(2):
-        cols = slice(h * 512, (h + 1) * 512)
-        att[:, h * HD:(h + 1) * HD] = (acc[:, cols] / den[:, cols]).T.astype(BF16)
-
+        if dx == 0:
+            for d in (1, 3, 2):
+                z2 = lax.rem(zz + d, 4)
+                wait_bytes(w_buf.at[w_rows(z2, mine16, 16)], wx_recv.at[z2])
+                for ex in (1, 3, 2):
+                    peer = 2 * lax.rem(xx + ex, 4) + core
+                    remote(w_buf.at[w_rows(z2, mine16, 16)], w_buf.at[w_rows(z2, mine16, 16)],
+                           w_send, wf_recv.at[z2], head, peer)
+
+    for n in range(8):
+        cols = slice(n * HD, (n + 1) * HD)
+        att[:, cols] = (acc[:, cols] / den[:, cols]).T.astype(BF16)
+
+    for d in (1, 3, 2):
+        z2 = lax.rem(zz + d, 4)
+        wait_bytes(w_buf.at[w_rows(z2, 0, 48)], wf_recv.at[z2])
+        here = w_rows(z2, 128 + core * 64, 64)
+        remote(w_buf.at[here], w_buf.at[here], w_send, ws_recv.at[z2, 1], head, sibling)
+    for d in (1, 3, 2):
+        z2 = lax.rem(zz + d, 4)
+        here = w_rows(z2, core * 64, 64)
+        wait_bytes(w_buf.at[here], wz_recv.at[z2])
+        remote(w_buf.at[here], w_buf.at[here], w_send, ws_recv.at[z2, 0], head, sibling)
+    for d in (1, 3, 2):
+        z2 = lax.rem(zz + d, 4)
+        for i in range(2):
+            wait_bytes(w_buf.at[w_rows(z2, i * 128 + (1 - core) * 64, 64)], ws_recv.at[z2, i])
     w_copy.wait()
-    for d in (2, 1, 3, 0):
-        z2, y2 = lax.rem(zz + d, 4), lax.rem(yy + d, 4)
-        a0 = jnp.concatenate(
-            [att[pl.ds(pl.multiple_of((i * 4 + z2) * 32, 32), 32), :] for i in range(4)], axis=0
-        )
-        part[0, z2] = dot(a0, w_buf[:, :HALF]).astype(BF16)
-        if d:
-            remote(part.at[0, z2], got.at[0, zz], send1, recv1.at[0, zz], yy * 4 + z2, qblk)
-        a1 = att[pl.ds(pl.multiple_of(y2 * 128, 128), 128), :]
-        part[1, y2] = dot(a1, w_buf[:, HALF:]).astype(BF16)
-        if d:
-            remote(part.at[1, y2], got.at[1, yy], send1, recv1.at[1, yy], y2 * 4 + zz, qblk)
-
-    sum0 = part[0, zz].astype(F32)
-    sum1 = part[1, yy].astype(F32)
-    for d in (1, 3, 2):
-        z2, y2 = lax.rem(zz + d, 4), lax.rem(yy + d, 4)
-        wait_bytes(got.at[0, z2], recv1.at[0, z2])
-        sum0 += got[0, z2].astype(F32)
-        wait_bytes(got.at[1, y2], recv1.at[1, y2])
-        sum1 += got[1, y2].astype(F32)
-    mid[0] = sum0.reshape(4, 32, HALF).astype(BF16)
-    mid[1] = sum1.reshape(4, 32, HALF).astype(BF16)
-    for d in (2, 1, 3):
-        z2, y2 = lax.rem(zz + d, 4), lax.rem(yy + d, 4)
-        remote(mid.at[0, y2], got2.at[0, yy], send2, recv2.at[0, yy], y2 * 4 + zz, qblk)
-        remote(mid.at[1, z2], got2.at[1, zz], send2, recv2.at[1, zz], yy * 4 + z2, qblk)
-    h0 = res_ref[:, :HALF].astype(F32) + mid[0, yy].astype(F32)
-    h1 = res_ref[:, HALF:].astype(F32) + mid[1, zz].astype(F32)
-    for d in (1, 3, 2):
-        z2, y2 = lax.rem(zz + d, 4), lax.rem(yy + d, 4)
-        wait_bytes(got2.at[0, y2], recv2.at[0, y2])
-        h0 += got2[0, y2].astype(F32)
-        wait_bytes(got2.at[1, z2], recv2.at[1, z2])
-        h1 += got2[1, z2].astype(F32)
-    square = jnp.sum(h0 * h0, axis=1, keepdims=True) + jnp.sum(h1 * h1, axis=1, keepdims=True)
+
+    for n in range(4):
+        part[n] = dot(att[...], w_buf[:, n * 512:(n + 1) * 512]).reshape(4, 32, 512).astype(BF16)
+        for d in (2, 1, 3):
+            y2 = lax.rem(yy + d, 4)
+            remote(part.at[n, y2], got.at[n, yy], send1, recv1.at[yy], y2 * 4 + zz, qblk)
+
+    h = [
+        res_ref[:, n * 512:(n + 1) * 512].astype(F32) + part[n, yy].astype(F32) for n in range(4)
+    ]
+    for d in (1, 3, 2):
+        y2 = lax.rem(yy + d, 4)
+        wait_bytes(got.at[:, y2], recv1.at[y2])
+        h = [h[n] + got[n, y2].astype(F32) for n in range(4)]
+    square = sum(jnp.sum(v * v, axis=1, keepdims=True) for v in h)
     rs = lax.rsqrt(square * (1.0 / D) + 1e-6)
-    hid[:, :HALF] = h0
-    hid[:, HALF:] = h1
-    n0 = (h0 * rs * gain_ref[:, :HALF]).astype(BF16)
-    n1 = (h1 * rs * gain_ref[:, HALF:]).astype(BF16)
-    for c, n in enumerate((n0, n1)):
-        for half in range(2):
-            x4[(2 * c + half) * 32:(2 * c + half + 1) * 32, :] = n[:, half * 512:(half + 1) * 512]
+    for n in range(4):
+        f = slice(n * 512, (n + 1) * 512)
+        hid[:, f] = h[n]
+        x4[n * 32:(n + 1) * 32, :] = (h[n] * rs * gain_ref[:, f]).astype(BF16)
     pl.semaphore_wait(all_sem, 3)
 
     outbox[...] = dot(pick[...], x4[...]).astype(BF16)
@@ -290,8 +314,9 @@
         f = slice(c * 512, (c + 1) * 512)
         out_ref[:, f] = (hid[:, f] + total[c * 32:(c + 1) * 32]).astype(BF16)
     wait_bytes(kv.at[pl.ds(0, 7)], kv_send)
+    wait_bytes(q_buf.at[pl.ds(0, 3)], q_send)
+    wait_bytes(w_buf.at[pl.ds(0, 768)], w_send)
     wait_bytes(part.at[:, pl.ds(0, 3)], send1)
-    wait_bytes(mid.at[:, pl.ds(0, 3)], send2)
     wait_bytes(outbox.at[pl.ds(0, 127 * 16)], send3)
     wait_bytes(ybox.at[pl.ds(0, 127 * 16)], send4)
 
@@ -305,21 +330,20 @@
     return pl.pallas_call(
         layer_kernel,
         out_shape=jax.ShapeDtypeStruct((32, D), BF16),
-        in_specs=[vmem, hbm, hbm, vmem, vmem, vmem, vmem, vmem, hbm, hbm, hbm, hbm],
+        in_specs=[hbm, hbm, hbm, vmem, vmem, vmem, vmem, vmem, hbm, hbm, hbm, hbm],
         out_specs=vmem,
         scratch_shapes=[
             scratch((8, 2, 256, HD), BF16),
-            scratch((256, D), BF16),
+            scratch((4, 4, 32, 2 * HD), BF16),
+            scratch((1024, D), BF16),
             scratch((HD, 512), BF16),
             scratch((1, 1024), F32),
             scratch((1, 1024), F32),
             scratch((HD, 1024), F32),
-            scratch((512, 256), BF16),
-            scratch((2, 4, 128, HALF), BF16),
-            scratch((2, 4, 128, HALF), BF16),
-            scratch((2, 4, 32, HALF), BF16),
-            scratch((2, 4, 32, HALF), BF16),
-            dma, dma, dma, dma((8,)), dma, dma((2, 4)), dma, dma((2, 4)),
+            scratch((128, 1024), BF16),
+            scratch((4, 4, 32, 512), BF16),
+            scratch((4, 4, 32, 512), BF16),
+            dma, dma, dma, dma((8,)), dma, dma((4,)), dma, dma((4,)), dma((4,)), dma((4,)), dma((4, 2)), dma, dma((4,)),
             scratch((D, FF), BF16),
             scratch((D, FF), BF16),
             scratch((FF, D), BF16),
@@ -341,7 +365,7 @@
         ),
         name="layer",
     )(
-        queries, key_cache, value_cache, visible_len.reshape(1, -1), residual,
+        queries.reshape(4, 4, 32, 2 * HD), key_cache, value_cache, visible_len.reshape(1, -1), residual,
         norm_gain.reshape(1, -1), expert_ids.T, route_weights.T, out_weight, w_gate, w_up, w_down,
     )
 

time: 98.3 us -> 90.8 us (0.924)
  Pallas kernels: 96.6 us -> 88.2 us
    pallas_call x1, Pallas kernels: 96.6 us -> 88.2 us  [per_device(): pl.pallas_call(layer_kernel, out_shape=jax.ShapeDtypeStruct((32, D), BF16...]
where the time goes in v3:
time: 90.8 us; the launch traced here: 89.7 us
  Pallas kernels  88.2 us (97%)
  local copies, waits for them, and re-layouts  1.57 us (2%)
    pallas_call x1, Pallas kernels, per_device(): pl.pallas_call(layer_kernel, out_shape=jax.ShapeDtypeStruct((32, D), BF16...  88.2 us

profile of v3, /device:TPU:1, one launch (start us, length us, event | category | flops | bytes accessed | tf_op | source)
XLA Modules:
  0.0 89.7 jit_solution(927064943404343335)
XLA Ops:
  0.0 88.2 %layer.1 = bf16[32,2048]{1,0:T(8,128)(2,1)} custom-call(bf16[4,4,32,256]{3,2,1,0:T(8,128)(2,1)} %bitcast.5, bf16[4,256,128]{2,1,0:T(8,128)(2,1)} %key_ref.1, bf16[4,256,128]{2,1,0:T(8,128)(2,1)} %value_ref.1, s32[1,512]{1,0:T(1,128)} %bitcast.9, bf16[32,2048]{1,0:T(8,128)(2,1)} %res_ref.1, f32[1,2048]{1,0:T(1,128)} %bitcast.6, s32[8,32]{1,0:T(8,128)} %bitcast.7, ...), custom_call_target="tpu_custom_call" | custom-call | tf_op jit(solution)/shard_map/layer/pallas_call | solution.py:330
  88.2 1.6 %copy.14 = bf16[32,2048]{1,0:T(8,128)(2,1)} copy(bf16[32,2048]{1,0:T(8,128)(2,1)} %layer.1) | data formatting | bytes 262144

commit v4 on v3

--- a/solution.py
+++ b/solution.py
@@ -11,7 +11,8 @@
 HD = 128
 FF = 768
 NEG = -1e30
-STRIDE = 37
+WIDTH = (640, 640, 768)
+FEATURES = (slice(0, 640), slice(640, 1280), slice(1280, 2048))
 QSCALE = HD ** (-0.5) * 1.4426950408889634
 VMEM_LIMIT = 58 * 1024 * 1024
 
@@ -40,49 +41,88 @@
     return pl.ds(pl.multiple_of(i * 16, 16), 16)
 
 
-def route(ids_ref, rw_ref, pick, mix):
-    expert = iota((128, 32), 0)
-    named = jnp.zeros((128, 32), F32)
-    weight = jnp.zeros((128, 32), F32)
+def offsets(m):
+    e = ((m & 15) * 5) & 15
+    return e >> 2, e & 3
+
+
+def partner(axis, head, qblk, m, sign):
+    p, q = offsets(m)
+    x, y, z = qblk >> 1, head >> 2, head & 3
+    if axis == 0:
+        y, z = (y + sign * p) & 3, (z + sign * q) & 3
+    elif axis == 1:
+        x, z = (x + sign * p) & 3, (z + sign * q) & 3
+    else:
+        x, y = (x + sign * p) & 3, (y + sign * q) & 3
+    return y * 4 + z, x * 2 + ((qblk + (m >> 4)) & 1)
+
+
+def source(axis, head, qblk, row):
+    p, q = offsets(row >> 4)
+    i = (row >> 2) & 3
+    x, y, z = qblk >> 1, head >> 2, head & 3
+    if axis == 0:
+        x, y, z = i, (y - p) & 3, (z - q) & 3
+    elif axis == 1:
+        x, y, z = (x - p) & 3, i, (z - q) & 3
+    else:
+        x, y, z = (x - p) & 3, (y - q) & 3, i
+    return x * 64 + y * 16 + z * 4 + (row & 3)
+
+
+def one_hot(hit):
+    return jnp.where(hit, 1.0, 0.0).astype(BF16)
+
+
+def route(axis, head, qblk, info, pick, mix):
+    line = info[axis, 0]
+    for i in range(1, 4):
+        line += pltpu.roll(info[axis, i], 32 * i, 1)
+    expert = iota((128, 128), 0).astype(F32)
+    token = iota((128, 128), 1)
+    named = jnp.zeros((128, 128), F32)
+    weight = jnp.zeros((128, 128), F32)
     for k in range(8):
-        hit = ids_ref[k:k + 1, :] == expert
+        hit = line[k:k + 1] == expert
         named = jnp.where(hit, 1.0, named)
-        weight = jnp.where(hit, rw_ref[k:k + 1, :], weight)
-    later = jnp.where(iota((32, 32), 0) < iota((32, 32), 1), 1.0, 0.0).astype(BF16)
+        weight = jnp.where(hit, line[8 + k:9 + k], weight)
+    before = iota((128, 128), 0)
+    later = one_hot((before < token) & (before >> 5 == token >> 5))
     rank = jnp.where(named > 0.0, dot(named.astype(BF16), later), -1.0)
-    four = jnp.where(iota((32, 128), 0) == lax.rem(iota((32, 128), 1), 32), 1.0, 0.0).astype(BF16)
-    rank4 = dot(rank.astype(BF16), four)
     high = weight.astype(BF16)
     low = (weight - high.astype(F32)).astype(BF16)
-
-    spread = jnp.where(iota((2048, 128), 0) // 16 == iota((2048, 128), 1), 1.0, 0.0).astype(BF16)
-    at = dot(spread, rank4.astype(BF16))
-    j = iota((2048, 128), 0)
-    take = (at == lax.rem(j, 4).astype(F32)) & (lax.rem(j // 4, 4) == iota((2048, 128), 1) // 32)
-    pick[...] = jnp.where(take, 1.0, 0.0).astype(BF16)
-
-    spread_t = jnp.where(iota((128, 2048), 1) // 16 == iota((128, 2048), 0), 1.0, 0.0).astype(BF16)
-    at_t = dot(rank4.T.astype(BF16), spread_t)
-    jt = iota((128, 2048), 1)
-    take_t = (at_t == lax.rem(jt, 4).astype(F32)) & (lax.rem(jt // 4, 4) == iota((128, 2048), 0) // 32)
+    m_head, m_qblk = partner(axis, head, qblk, iota((32, 128), 0), 1)
+    order = one_hot(m_head * 8 + m_qblk == iota((32, 128), 1))
+    rank = dot(order, rank.astype(BF16))
+
+    j = iota((512, 128), 0)
+    at = dot(one_hot(iota((512, 32), 0) >> 4 == iota((512, 32), 1)), rank.astype(BF16))
+    take = (at == (j & 3).astype(F32)) & ((j >> 2) & 3 == iota((512, 128), 1) >> 5)
+    pick[axis] = one_hot(take)
+    spread = one_hot(iota((32, 512), 1) >> 4 == iota((32, 512), 0))
+    j = iota((128, 512), 1)
+    at = dot(rank.T.astype(BF16), spread)
+    take = (at == (j & 3).astype(F32)) & ((j >> 2) & 3 == iota((128, 512), 0) >> 5)
     for i, w in enumerate((high, low)):
-        w4 = dot(dot(w, four).T.astype(BF16), spread_t)
-        mix[i] = jnp.where(take_t, w4, 0.0).astype(BF16)
+        w = dot(dot(order, w).T.astype(BF16), spread)
+        mix[axis, i] = jnp.where(take, w, 0.0).astype(BF16)
 
 
 def layer_kernel(
     q_ref, key_ref, value_ref, vis_ref, res_ref, gain_ref, ids_ref, rw_ref, w_ref, wg_ref, wu_ref, wd_ref,
     out_ref,
-    kv, q_buf, w_buf, vt, top, den, acc, att, part, got,
+    kv, q_buf, w_buf, vt, top, den, acc, att, total, part, got,
     own_sem, w_sem, kv_send, kv_recv, q_send, q_recv, w_send, wz_recv, wx_recv, wf_recv, ws_recv, send1, recv1,
-    wg, wu, wd, hid, x4, pick, outbox, inbox, ybox, backbox, mix, x_buf, y_buf,
-    e_sem, send3, recv3, send4, recv4, plane_sem, all_sem,
+    wg, wu, wd, hid, own_info, info, pick, mix, sort, unsort, x_buf, y_buf,
+    lines_x, lines_y, lines_z, out_x, out_y, out_z, in_x, in_y, in_z, ret_x, ret_y, ret_z, back_x, back_y, back_z,
+    sum_x, sum_y, sum_z, got_x, got_y, got_z,
+    e_sem, info_send, info_recv, line_send, line_recv, send3, recv3, send4, recv4, sum_send, sum_recv, plane_sem, all_sem,
 ):
     head, qblk = lax.axis_index("head"), lax.axis_index("qblk")
     yy, zz = head // 4, lax.rem(head, 4)
     xx, core = qblk // 2, lax.rem(qblk, 2)
     sibling = 2 * xx + 1 - core
-    me = head * 8 + qblk
 
     def remote(src, dst, ssem, rsem, h, q):
         c = pltpu.make_async_remote_copy(
@@ -98,6 +138,17 @@
     z_line = [(yy * 4 + lax.rem(zz + d, 4), qblk) for d in (1, 3, 2)]
     x_line = [(head, lax.rem(qblk + d, 8)) for d in range(1, 8)]
 
+    place = (xx, yy, zz)
+    peers = (
+        [(head, 2 * lax.rem(xx + d, 4) + core) for d in (1, 3, 2)], y_line, z_line,
+    )
+    lines, outbox, inbox = (lines_x, lines_y, lines_z), (out_x, out_y, out_z), (in_x, in_y, in_z)
+    ybox, backbox = (ret_x, ret_y, ret_z), (back_x, back_y, back_z)
+    sums, others = (sum_x, sum_y, sum_z), (got_x, got_y, got_z)
+
+    def rows32(i):
+        return pl.ds(pl.multiple_of(i * 32, 32), 32)
+
     barrier = pltpu.get_barrier_semaphore()
     for h, q in x_line + y_line + z_line:
         signal(barrier, h, q)
@@ -111,6 +162,12 @@
         for dx in (1, 3, 2):
             peer = 2 * lax.rem(xx + dx, 4) + core
             remote(src.at[yy], kv.at[qblk, j], kv_send, kv_recv.at[qblk], head, peer)
+    own = jnp.concatenate([ids_ref[...].astype(F32), rw_ref[...]], axis=0)
+    own_info[...] = jnp.concatenate([own, jnp.zeros((16, 96), F32)], axis=1)
+    for a in range(3):
+        info[a, place[a]] = own_info[...]
+        for h, q in peers[a]:
+            remote(own_info, info.at[a, place[a]], info_send, info_recv.at[a], h, q)
     def w_rows(z, first, count):
         return pl.ds(pl.multiple_of(z * 256 + first, 16), count)
 
@@ -136,7 +193,11 @@
     ]
     for c in w_copies:
         c.start()
-    route(ids_ref, rw_ref, pick, mix)
+    for a in range(3):
+        wait_bytes(info.at[a, pl.ds(0, 3)], info_recv.at[a])
+        route(a, head, qblk, info, pick, mix)
+        sort[a] = one_hot(source(a, head, qblk, iota((256, 256), 1)) == iota((256, 256), 0))
+        unsort[a] = one_hot(source(a, head, qblk, iota((256, 256), 0)) == iota((256, 256), 1))
     pl.semaphore_wait(plane_sem, 3)
     for h, q in z_line:
         signal(all_sem, h, q)
@@ -184,7 +245,7 @@
             acc[:, cols] = acc[:, cols] * scale + dot(vt[...], p.astype(BF16))
             return carry
 
-        lax.fori_loop(0, 4, rows, 0)
+        lax.fori_loop(0, 4, rows, 0, unroll=True)
 
         if dx == 0:
             for d in (1, 3, 2):
@@ -197,26 +258,35 @@
 
     for n in range(8):
         cols = slice(n * HD, (n + 1) * HD)
-        att[:, cols] = (acc[:, cols] / den[:, cols]).T.astype(BF16)
-
+        att[n // 2, :, (n % 2) * HD:(n % 2 + 1) * HD] = (acc[:, cols] / den[:, cols]).T.astype(BF16)
+
+    for d in (1, 3):
+        z2 = lax.rem(zz + d, 4)
+        here = w_rows(z2, core * 64, 64)
+        wait_bytes(w_buf.at[here], wz_recv.at[z2])
+        remote(w_buf.at[here], w_buf.at[here], w_send, ws_recv.at[z2, 0], head, sibling)
     for d in (1, 3, 2):
         z2 = lax.rem(zz + d, 4)
         wait_bytes(w_buf.at[w_rows(z2, 0, 48)], wf_recv.at[z2])
         here = w_rows(z2, 128 + core * 64, 64)
         remote(w_buf.at[here], w_buf.at[here], w_send, ws_recv.at[z2, 1], head, sibling)
-    for d in (1, 3, 2):
-        z2 = lax.rem(zz + d, 4)
-        here = w_rows(z2, core * 64, 64)
-        wait_bytes(w_buf.at[here], wz_recv.at[z2])
-        remote(w_buf.at[here], w_buf.at[here], w_send, ws_recv.at[z2, 0], head, sibling)
+    z2 = lax.rem(zz + 2, 4)
+    here = w_rows(z2, core * 64, 64)
+    wait_bytes(w_buf.at[here], wz_recv.at[z2])
+    remote(w_buf.at[here], w_buf.at[here], w_send, ws_recv.at[z2, 0], head, sibling)
+
+    w_copy.wait()
+    total[...] = dot(att[zz], w_buf[w_rows(zz, 0, 256), :])
     for d in (1, 3, 2):
         z2 = lax.rem(zz + d, 4)
         for i in range(2):
             wait_bytes(w_buf.at[w_rows(z2, i * 128 + (1 - core) * 64, 64)], ws_recv.at[z2, i])
-    w_copy.wait()
-
+        if d != 2:
+            total[...] += dot(att[z2], w_buf[w_rows(z2, 0, 256), :])
     for n in range(4):
-        part[n] = dot(att[...], w_buf[:, n * 512:(n + 1) * 512]).reshape(4, 32, 512).astype(BF16)
+        f = slice(n * 512, (n + 1) * 512)
+        last = total[:, f] + dot(att[z2], w_buf[w_rows(z2, 0, 256), f])
+        part[n] = last.reshape(4, 32, 512).astype(BF16)
         for d in (2, 1, 3):
             y2 = lax.rem(yy + d, 4)
             remote(part.at[n, y2], got.at[n, yy], send1, recv1.at[yy], y2 * 4 + zz, qblk)
@@ -231,94 +301,87 @@
     square = sum(jnp.sum(v * v, axis=1, keepdims=True) for v in h)
     rs = lax.rsqrt(square * (1.0 / D) + 1e-6)
     for n in range(4):
-        f = slice(n * 512, (n + 1) * 512)
-        hid[:, f] = h[n]
-        x4[n * 32:(n + 1) * 32, :] = (h[n] * rs * gain_ref[:, f]).astype(BF16)
+        hid[:, n * 512:(n + 1) * 512] = h[n]
+    for a, f in enumerate(FEATURES):
+        here = lines[a].at[rows32(place[a])]
+        here[...] = (hid[:, f] * rs * gain_ref[:, f]).astype(BF16)
+        for h, q in peers[a]:
+            remote(here, here, line_send.at[a], line_recv.at[a], h, q)
     pl.semaphore_wait(all_sem, 3)
-
-    outbox[...] = dot(pick[...], x4[...]).astype(BF16)
-
-
-    def partner(k, sign):
-        d = lax.rem(k * STRIDE, 128)
-        py = lax.rem(head // 4 + sign * (d // 32) + 4, 4)
-        pz = lax.rem(lax.rem(head, 4) + sign * lax.rem(d // 8, 4) + 4, 4)
-        px = lax.rem(qblk // 2 + sign * lax.rem(d // 2, 4) + 4, 4)
-        return py * 4 + pz, px * 2 + lax.rem(lax.rem(qblk, 2) + lax.rem(d, 2), 2)
-
-    def dispatch(k, carry):
-        eh, eq = partner(k, 1)
-        pltpu.make_async_remote_copy(
-            src_ref=outbox.at[rows16(eh * 8 + eq)], dst_ref=inbox.at[rows16(k)],
-            send_sem=send3, recv_sem=recv3.at[k // 32],
-            device_id=(eh, eq), device_id_type=MESH,
-        ).start()
+    for a in range(3):
+        wait_bytes(lines[a].at[pl.ds(0, 96)], line_recv.at[a])
+
+    def dispatch(m, carry):
+        for a in range(3):
+            h, q = partner(a, head, qblk, m, 1)
+            remote(outbox[a].at[rows16(m)], inbox[a].at[rows16(m)], send3.at[a], recv3.at[a, m // 16], h, q)
         return carry
 
-    lax.fori_loop(1, 128, dispatch, 0)
-    pltpu.make_async_copy(outbox.at[rows16(me)], inbox.at[rows16(0)], recv3.at[0]).start()
-
-    r, col = iota((128, 128), 0), iota((128, 128), 1)
-    source_row = (lax.rem(r, 32) // 4) * 16 + (r // 32) * 4 + lax.rem(r, 4)
-    sort = jnp.where(col == source_row, 1.0, 0.0).astype(BF16)
-    c_row = (lax.rem(r, 16) // 4) * 32 + (r // 16) * 4 + lax.rem(r, 4)
-    unsort = jnp.where(col == c_row, 1.0, 0.0).astype(BF16)
+    for r in range(2):
+        block = pl.ds(r * 256, 256)
+        for a in range(3):
+            outbox[a][block] = dot(pick[a, block], lines[a][...]).astype(BF16)
+            if r == 0:
+                pltpu.make_async_copy(outbox[a].at[rows16(0)], inbox[a].at[rows16(0)], recv3.at[a, 0]).start()
+        lax.fori_loop(max(r * 16, 1), r * 16 + 16, dispatch, 0)
 
     for c in w_copies:
         c.wait()
 
-    def one_round(rnd, carry):
-        block = pl.ds(pl.multiple_of(rnd * 512, 512), 512)
-        wait_bytes(inbox.at[block], recv3.at[rnd])
-        for i in range(4):
-            x = dot(sort, inbox[pl.ds(pl.multiple_of(rnd * 512 + i * 128, 128), 128), :]).astype(BF16)
-            for c in range(4):
-                x_buf[i * 32:(i + 1) * 32, c * 512:(c + 1) * 512] = x[c * 32:(c + 1) * 32]
+    def one_round(r, carry):
+        block = pl.ds(pl.multiple_of(r * 256, 256), 256)
+        for a, f in enumerate(FEATURES):
+            wait_bytes(inbox[a].at[block], recv3.at[a, r])
+            x_buf[:, f] = dot(sort[a], inbox[a][block]).astype(BF16)
         gate = dot(x_buf[...], wg[...])
         up = dot(x_buf[...], wu[...])
         hidden = (gate / (1.0 + jnp.exp(-gate)) * up).astype(BF16)
         y_buf[...] = dot(hidden, wd[...]).astype(BF16)
-        for i in range(4):
-            y = jnp.concatenate(
-                [y_buf[i * 32:(i + 1) * 32, c * 512:(c + 1) * 512] for c in range(4)], axis=0
-            )
-            ybox[pl.ds(pl.multiple_of(rnd * 512 + i * 128, 128), 128), :] = dot(unsort, y).astype(BF16)
-
-        def send_back(k, carry):
-            p = rnd * 32 + k
-            sh, sq = partner(p, -1)
-            remote = p != 0
-
-            @pl.when(remote)
-            def _():
-                pltpu.make_async_remote_copy(
-                    src_ref=ybox.at[rows16(p)], dst_ref=backbox.at[rows16(me)],
-                    send_sem=send4, recv_sem=recv4,
-                    device_id=(sh, sq), device_id_type=MESH,
-                ).start()
-
-            @pl.when(jnp.logical_not(remote))
-            def _():
-                pltpu.make_async_copy(ybox.at[rows16(p)], backbox.at[rows16(me)], recv4).start()
-
+        for a, f in enumerate(FEATURES):
+            ybox[a][block] = dot(unsort[a], y_buf[:, f]).astype(BF16)
+
+        def send_back(m, carry):
+            for a in range(3):
+                h, q = partner(a, head, qblk, m, -1)
+                remote(ybox[a].at[rows16(m)], backbox[a].at[rows16(m)], send4.at[a], recv4.at[a, r], h, q)
             return carry
 
-        lax.fori_loop(0, 32, send_back, 0)
+        @pl.when(r == 0)
+        def _():
+            for a in range(3):
+                pltpu.make_async_copy(ybox[a].at[rows16(0)], backbox[a].at[rows16(0)], recv4.at[a, 0]).start()
+
+        lax.fori_loop(jnp.maximum(r * 16, 1), r * 16 + 16, send_back, 0)
         return carry
 
-    lax.fori_loop(0, 4, one_round, 0)
-
-    wait_bytes(backbox, recv4)
-    total = dot(mix[0], backbox[...]) + dot(mix[1], backbox[...])
-    for c in range(4):
-        f = slice(c * 512, (c + 1) * 512)
-        out_ref[:, f] = (hid[:, f] + total[c * 32:(c + 1) * 32]).astype(BF16)
+    lax.fori_loop(0, 2, one_round, 0)
+
+    for a in range(3):
+        mixed = jnp.zeros((128, WIDTH[a]), F32)
+        for r in range(2):
+            block = slice(r * 256, (r + 1) * 256)
+            wait_bytes(backbox[a].at[block], recv4.at[a, r])
+            mixed += dot(mix[a, 0, :, block], backbox[a][block]) + dot(mix[a, 1, :, block], backbox[a][block])
+        sums[a][...] = mixed.astype(BF16)
+        for d, (h, q) in zip((1, 3, 2), peers[a]):
+            remote(sums[a].at[rows32(lax.rem(place[a] + d, 4))], others[a].at[rows32(place[a])],
+                   sum_send.at[a], sum_recv.at[a], h, q)
+    for a, f in enumerate(FEATURES):
+        v = hid[:, f] + sums[a][rows32(place[a])].astype(F32)
+        wait_bytes(others[a].at[pl.ds(0, 96)], sum_recv.at[a])
+        for d in (1, 3, 2):
+            v += others[a][rows32(lax.rem(place[a] + d, 4))].astype(F32)
+        out_ref[:, f] = v.astype(BF16)
     wait_bytes(kv.at[pl.ds(0, 7)], kv_send)
     wait_bytes(q_buf.at[pl.ds(0, 3)], q_send)
     wait_bytes(w_buf.at[pl.ds(0, 768)], w_send)
     wait_bytes(part.at[:, pl.ds(0, 3)], send1)
-    wait_bytes(outbox.at[pl.ds(0, 127 * 16)], send3)
-    wait_bytes(ybox.at[pl.ds(0, 127 * 16)], send4)
+    wait_bytes(info.at[:, pl.ds(0, 3)], info_send)
+    for a in range(3):
+        wait_bytes(lines[a].at[pl.ds(0, 96)], line_send.at[a])
+        wait_bytes(outbox[a].at[pl.ds(0, 31 * 16)], send3.at[a])
+        wait_bytes(ybox[a].at[pl.ds(0, 31 * 16)], send4.at[a])
+        wait_bytes(sums[a].at[pl.ds(0, 96)], sum_send.at[a])
 
 
 def per_device(
@@ -340,7 +403,8 @@
             scratch((1, 1024), F32),
             scratch((1, 1024), F32),
             scratch((HD, 1024), F32),
-            scratch((128, 1024), BF16),
+            scratch((4, 128, 2 * HD), BF16),
+            scratch((128, D), F32),
             scratch((4, 4, 32, 512), BF16),
             scratch((4, 4, 32, 512), BF16),
             dma, dma, dma, dma((8,)), dma, dma((4,)), dma, dma((4,)), dma((4,)), dma((4,)), dma((4, 2)), dma, dma((4,)),
@@ -348,16 +412,16 @@
             scratch((D, FF), BF16),
             scratch((FF, D), BF16),
             scratch((32, D), F32),
-            scratch((128, 512), BF16),
-            scratch((2048, 128), BF16),
-            scratch((2048, 512), BF16),
-            scratch((2048, 512), BF16),
-            scratch((2048, 512), BF16),
-            scratch((2048, 512), BF16),
-            scratch((2, 128, 2048), BF16),
-            scratch((128, D), BF16),
-            scratch((128, D), BF16),
-            dma((3,)), dma, dma((4,)), dma, dma,
+            scratch((16, 128), F32),
+            scratch((3, 4, 16, 128), F32),
+            scratch((3, 512, 128), BF16),
+            scratch((3, 2, 128, 512), BF16),
+            scratch((3, 256, 256), BF16),
+            scratch((3, 256, 256), BF16),
+            scratch((256, D), BF16),
+            scratch((256, D), BF16),
+            *[scratch((rows, w), BF16) for rows in (128, 512, 512, 512, 512, 128, 128) for w in WIDTH],
+            dma((3,)), dma, dma((3,)), dma((3,)), dma((3,)), dma((3,)), dma((3, 2)), dma((3,)), dma((3, 2)), dma((3,)), dma((3,)),
             pltpu.SemaphoreType.REGULAR, pltpu.SemaphoreType.REGULAR,
         ],
         compiler_params=pltpu.CompilerParams(

time: 90.8 us -> 90 us (level)
  no operation moved by 1% of the time
where the time goes in v4:
time: 90 us; the launch traced here: 89.6 us
  Pallas kernels  88.1 us (98%)
  local copies, waits for them, and re-layouts  1.57 us (2%)
    pallas_call x1, Pallas kernels, per_device(): pl.pallas_call(layer_kernel, out_shape=jax.ShapeDtypeStruct((32, D), BF16...  88.1 us

profile of v4, /device:TPU:1, one launch (start us, length us, event | category | flops | bytes accessed | tf_op | source)
XLA Modules:
  0.0 89.6 jit_solution(5355662841533141232)
XLA Ops:
  0.0 88.1 %layer.1 = bf16[32,2048]{1,0:T(8,128)(2,1)} custom-call(bf16[4,4,32,256]{3,2,1,0:T(8,128)(2,1)} %bitcast.5, bf16[4,256,128]{2,1,0:T(8,128)(2,1)} %key_ref.1, bf16[4,256,128]{2,1,0:T(8,128)(2,1)} %value_ref.1, s32[1,512]{1,0:T(1,128)} %bitcast.9, bf16[32,2048]{1,0:T(8,128)(2,1)} %res_ref.1, f32[1,2048]{1,0:T(1,128)} %bitcast.6, s32[8,32]{1,0:T(8,128)} %bitcast.7, ...), custom_call_target="tpu_custom_call" | custom-call | tf_op jit(solution)/shard_map/layer/pallas_call | solution.py:393
  88.1 1.6 %copy.14 = bf16[32,2048]{1,0:T(8,128)(2,1)} copy(bf16[32,2048]{1,0:T(8,128)(2,1)} %layer.1) | data formatting | bytes 262144

commit v5 on v4

--- a/solution.py
+++ b/solution.py
@@ -75,7 +75,7 @@
     return jnp.where(hit, 1.0, 0.0).astype(BF16)
 
 
-def route(axis, head, qblk, info, pick, mix):
+def route(axis, head, qblk, info, pick, tab):
     line = info[axis, 0]
     for i in range(1, 4):
         line += pltpu.roll(info[axis, i], 32 * i, 1)
@@ -100,12 +100,18 @@
     at = dot(one_hot(iota((512, 32), 0) >> 4 == iota((512, 32), 1)), rank.astype(BF16))
     take = (at == (j & 3).astype(F32)) & ((j >> 2) & 3 == iota((512, 128), 1) >> 5)
     pick[axis] = one_hot(take)
+    tab[axis, 0] = rank
+    for i, w in enumerate((high, low)):
+        tab[axis, 1 + i] = dot(order, w)
+
+
+def route_back(axis, tab, mix):
     spread = one_hot(iota((32, 512), 1) >> 4 == iota((32, 512), 0))
     j = iota((128, 512), 1)
-    at = dot(rank.T.astype(BF16), spread)
+    at = dot(tab[axis, 0].T.astype(BF16), spread)
     take = (at == (j & 3).astype(F32)) & ((j >> 2) & 3 == iota((128, 512), 0) >> 5)
-    for i, w in enumerate((high, low)):
-        w = dot(dot(order, w).T.astype(BF16), spread)
+    for i in range(2):
+        w = dot(tab[axis, 1 + i].T.astype(BF16), spread)
         mix[axis, i] = jnp.where(take, w, 0.0).astype(BF16)
 
 
@@ -114,7 +120,7 @@
     out_ref,
     kv, q_buf, w_buf, vt, top, den, acc, att, total, part, got,
     own_sem, w_sem, kv_send, kv_recv, q_send, q_recv, w_send, wz_recv, wx_recv, wf_recv, ws_recv, send1, recv1,
-    wg, wu, wd, hid, own_info, info, pick, mix, sort, unsort, x_buf, y_buf,
+    wg, wu, wd, hid, own_info, info, pick, tab, mix, sort, unsort, x_buf, y_buf,
     lines_x, lines_y, lines_z, out_x, out_y, out_z, in_x, in_y, in_z, ret_x, ret_y, ret_z, back_x, back_y, back_z,
     sum_x, sum_y, sum_z, got_x, got_y, got_z,
     e_sem, info_send, info_recv, line_send, line_recv, send3, recv3, send4, recv4, sum_send, sum_recv, plane_sem, all_sem,
@@ -193,11 +199,6 @@
     ]
     for c in w_copies:
         c.start()
-    for a in range(3):
-        wait_bytes(info.at[a, pl.ds(0, 3)], info_recv.at[a])
-        route(a, head, qblk, info, pick, mix)
-        sort[a] = one_hot(source(a, head, qblk, iota((256, 256), 1)) == iota((256, 256), 0))
-        unsort[a] = one_hot(source(a, head, qblk, iota((256, 256), 0)) == iota((256, 256), 1))
     pl.semaphore_wait(plane_sem, 3)
     for h, q in z_line:
         signal(all_sem, h, q)
@@ -291,6 +292,10 @@
             y2 = lax.rem(yy + d, 4)
             remote(part.at[n, y2], got.at[n, yy], send1, recv1.at[yy], y2 * 4 + zz, qblk)
 
+    for a in range(3):
+        wait_bytes(info.at[a, pl.ds(0, 3)], info_recv.at[a])
+        route(a, head, qblk, info, pick, tab)
+
     h = [
         res_ref[:, n * 512:(n + 1) * 512].astype(F32) + part[n, yy].astype(F32) for n in range(4)
     ]
@@ -325,6 +330,10 @@
                 pltpu.make_async_copy(outbox[a].at[rows16(0)], inbox[a].at[rows16(0)], recv3.at[a, 0]).start()
         lax.fori_loop(max(r * 16, 1), r * 16 + 16, dispatch, 0)
 
+    for a in range(3):
+        sort[a] = one_hot(source(a, head, qblk, iota((256, 256), 1)) == iota((256, 256), 0))
+        unsort[a] = one_hot(source(a, head, qblk, iota((256, 256), 0)) == iota((256, 256), 1))
+        route_back(a, tab, mix)
     for c in w_copies:
         c.wait()
 
@@ -415,6 +424,7 @@
             scratch((16, 128), F32),
             scratch((3, 4, 16, 128), F32),
             scratch((3, 512, 128), BF16),
+            scratch((3, 3, 32, 128), F32),
             scratch((3, 2, 128, 512), BF16),
             scratch((3, 256, 256), BF16),
             scratch((3, 256, 256), BF16),

time: 90 us -> 87 us (0.967)
  Pallas kernels: 88.1 us -> 85.2 us
    pallas_call x1, Pallas kernels: 88.1 us -> 85.2 us  [per_device(): pl.pallas_call(layer_kernel, out_shape=jax.ShapeDtypeStruct((32, D), BF16...]
where the time goes in v5:
time: 87 us; the launch traced here: 86.8 us
  Pallas kernels  85.2 us (98%)
  local copies, waits for them, and re-layouts  1.57 us (2%)
    pallas_call x1, Pallas kernels, per_device(): pl.pallas_call(layer_kernel, out_shape=jax.ShapeDtypeStruct((32, D), BF16...  85.2 us

profile of v5, /device:TPU:1, one launch (start us, length us, event | category | flops | bytes accessed | tf_op | source)
XLA Modules:
  0.0 86.8 jit_solution(17401671263032907245)
XLA Ops:
  0.0 85.2 %layer.1 = bf16[32,2048]{1,0:T(8,128)(2,1)} custom-call(bf16[4,4,32,256]{3,2,1,0:T(8,128)(2,1)} %bitcast.5, bf16[4,256,128]{2,1,0:T(8,128)(2,1)} %key_ref.1, bf16[4,256,128]{2,1,0:T(8,128)(2,1)} %value_ref.1, s32[1,512]{1,0:T(1,128)} %bitcast.9, bf16[32,2048]{1,0:T(8,128)(2,1)} %res_ref.1, f32[1,2048]{1,0:T(1,128)} %bitcast.6, s32[8,32]{1,0:T(8,128)} %bitcast.7, ...), custom_call_target="tpu_custom_call" | custom-call | tf_op jit(solution)/shard_map/layer/pallas_call | solution.py:402
  85.2 1.6 %copy.14 = bf16[32,2048]{1,0:T(8,128)(2,1)} copy(bf16[32,2048]{1,0:T(8,128)(2,1)} %layer.1) | data formatting | bytes 262144

commit v6 on v5

--- a/solution.py
+++ b/solution.py
@@ -12,6 +12,7 @@
 FF = 768
 NEG = -1e30
 WIDTH = (640, 640, 768)
+FORWARD = (0, 3)
 FEATURES = (slice(0, 640), slice(640, 1280), slice(1280, 2048))
 QSCALE = HD ** (-0.5) * 1.4426950408889634
 VMEM_LIMIT = 58 * 1024 * 1024
@@ -116,9 +117,10 @@
 
 
 def layer_kernel(
-    q_ref, key_ref, value_ref, vis_ref, res_ref, gain_ref, ids_ref, rw_ref, w_ref, wg_ref, wu_ref, wd_ref,
+    q_ref, key_ref, value_ref, vis_in, res_in, gain_in, ids_in, rw_in, w_ref, wg_ref, wu_ref, wd_ref,
     out_ref,
-    kv, q_buf, w_buf, vt, top, den, acc, att, total, part, got,
+    vis_ref, res_ref, gain_ref, ids_ref, rw_ref, small_sem,
+    kv, q_buf, q_t, w_buf, vt, top, den, acc, att, total, part, got,
     own_sem, w_sem, kv_send, kv_recv, q_send, q_recv, w_send, wz_recv, wx_recv, wf_recv, ws_recv, send1, recv1,
     wg, wu, wd, hid, own_info, info, pick, tab, mix, sort, unsort, x_buf, y_buf,
     lines_x, lines_y, lines_z, out_x, out_y, out_z, in_x, in_y, in_z, ret_x, ret_y, ret_z, back_x, back_y, back_z,
@@ -158,6 +160,12 @@
     barrier = pltpu.get_barrier_semaphore()
     for h, q in x_line + y_line + z_line:
         signal(barrier, h, q)
+    smalls = [
+        pltpu.make_async_copy(src, dst, small_sem.at[i]) for i, (src, dst) in enumerate((
+            (ids_in, ids_ref), (rw_in, rw_ref), (vis_in, vis_ref), (res_in, res_ref), (gain_in, gain_ref)))
+    ]
+    for c in smalls:
+        c.start()
     pl.semaphore_wait(barrier, 13)
 
     for d in (1, 3, 2):
@@ -168,6 +176,8 @@
         for dx in (1, 3, 2):
             peer = 2 * lax.rem(xx + dx, 4) + core
             remote(src.at[yy], kv.at[qblk, j], kv_send, kv_recv.at[qblk], head, peer)
+    for c in smalls:
+        c.wait()
     own = jnp.concatenate([ids_ref[...].astype(F32), rw_ref[...]], axis=0)
     own_info[...] = jnp.concatenate([own, jnp.zeros((16, 96), F32)], axis=1)
     for a in range(3):
@@ -178,21 +188,20 @@
         return pl.ds(pl.multiple_of(z * 256 + first, 16), count)
 
     mine16 = 128 + core * 64 + xx * 16
-    for d in (1, 3, 2):
-        z2 = lax.rem(zz + d, 4)
-        remote(w_ref.at[w_rows(0, mine16, 16)], w_buf.at[w_rows(zz, mine16, 16)],
-               w_send, wx_recv.at[zz], yy * 4 + z2, qblk)
-    for d in (1, 3, 2):
-        z2 = lax.rem(zz + d, 4)
-        remote(w_ref.at[w_rows(0, core * 64, 64)], w_buf.at[w_rows(zz, core * 64, 64)],
-               w_send, wz_recv.at[zz], yy * 4 + z2, qblk)
+    half = (slice(0, 1024), slice(1024, 2048))
+    for c in range(2):
+        for first, count, sems in ((mine16, 16, wx_recv), (core * 64, 64, wz_recv)):
+            for d in (1, 3, 2):
+                z2 = lax.rem(zz + d, 4)
+                remote(w_ref.at[w_rows(0, first, count), half[c]], w_buf.at[c, w_rows(zz, first, count)],
+                       w_send, sems.at[c, zz], yy * 4 + z2, qblk)
     for j, src in enumerate((key_ref, value_ref)):
         pltpu.make_async_copy(src.at[yy], kv.at[qblk, j], own_sem).start()
     pltpu.make_async_copy(q_ref.at[:, zz], q_buf.at[zz], q_recv.at[zz]).start()
     for h, q in y_line:
         signal(plane_sem, h, q)
-    w_copy = pltpu.make_async_copy(w_ref, w_buf.at[w_rows(zz, 0, 256)], w_sem)
-    w_copy.start()
+    for c in range(2):
+        pltpu.make_async_copy(w_ref.at[:, half[c]], w_buf.at[c, w_rows(zz, 0, 256)], w_sem).start()
     w_copies = [
         pltpu.make_async_copy(src.at[0], dst, e_sem.at[i])
         for i, (src, dst) in enumerate(((wg_ref, wg), (wu_ref, wu), (wd_ref, wd)))
@@ -214,6 +223,9 @@
     for d in range(4):
         z2 = lax.rem(zz + d, 4)
         wait_bytes(q_buf.at[z2], q_recv.at[z2])
+        q = q_buf[z2].reshape(128, 2 * HD).astype(F32)
+        q_t[z2, :, :128] = q[:, :HD].T.astype(BF16)
+        q_t[z2, :, 128:] = q[:, HD:].T.astype(BF16)
 
     top[...] = jnp.full(top.shape, NEG, F32)
     den[...] = jnp.zeros(den.shape, F32)
@@ -232,10 +244,8 @@
         base = chip * 512
 
         def rows(i, carry, keys=keys, base=base):
-            q = q_buf[i].reshape(128, 2 * HD)
-            q = jnp.concatenate([q[:, :HD], q[:, HD:]], axis=0)
             cols = pl.ds(pl.multiple_of(i * 256, 256), 256)
-            s = dot_nt(keys, q)
+            s = dot(keys, q_t[i])
             s = jnp.where(iota(s.shape, 0) < seen_all - base, s, NEG)
             old = top[:, cols]
             new = jnp.maximum(old, jnp.max(s, axis=0, keepdims=True))
@@ -248,49 +258,44 @@
 
         lax.fori_loop(0, 4, rows, 0, unroll=True)
 
-        if dx == 0:
+        if dx in FORWARD:
+            c = FORWARD.index(dx)
             for d in (1, 3, 2):
                 z2 = lax.rem(zz + d, 4)
-                wait_bytes(w_buf.at[w_rows(z2, mine16, 16)], wx_recv.at[z2])
+                here = w_buf.at[c, w_rows(z2, mine16, 16)]
+                wait_bytes(here, wx_recv.at[c, z2])
                 for ex in (1, 3, 2):
                     peer = 2 * lax.rem(xx + ex, 4) + core
-                    remote(w_buf.at[w_rows(z2, mine16, 16)], w_buf.at[w_rows(z2, mine16, 16)],
-                           w_send, wf_recv.at[z2], head, peer)
+                    remote(here, here, w_send, wf_recv.at[c, z2], head, peer)
 
     for n in range(8):
         cols = slice(n * HD, (n + 1) * HD)
         att[n // 2, :, (n % 2) * HD:(n % 2 + 1) * HD] = (acc[:, cols] / den[:, cols]).T.astype(BF16)
 
-    for d in (1, 3):
-        z2 = lax.rem(zz + d, 4)
-        here = w_rows(z2, core * 64, 64)
-        wait_bytes(w_buf.at[here], wz_recv.at[z2])
-        remote(w_buf.at[here], w_buf.at[here], w_send, ws_recv.at[z2, 0], head, sibling)
-    for d in (1, 3, 2):
-        z2 = lax.rem(zz + d, 4)
-        wait_bytes(w_buf.at[w_rows(z2, 0, 48)], wf_recv.at[z2])
-        here = w_rows(z2, 128 + core * 64, 64)
-        remote(w_buf.at[here], w_buf.at[here], w_send, ws_recv.at[z2, 1], head, sibling)
-    z2 = lax.rem(zz + 2, 4)
-    here = w_rows(z2, core * 64, 64)
-    wait_bytes(w_buf.at[here], wz_recv.at[z2])
-    remote(w_buf.at[here], w_buf.at[here], w_send, ws_recv.at[z2, 0], head, sibling)
-
-    w_copy.wait()
-    total[...] = dot(att[zz], w_buf[w_rows(zz, 0, 256), :])
-    for d in (1, 3, 2):
-        z2 = lax.rem(zz + d, 4)
-        for i in range(2):
-            wait_bytes(w_buf.at[w_rows(z2, i * 128 + (1 - core) * 64, 64)], ws_recv.at[z2, i])
-        if d != 2:
-            total[...] += dot(att[z2], w_buf[w_rows(z2, 0, 256), :])
-    for n in range(4):
-        f = slice(n * 512, (n + 1) * 512)
-        last = total[:, f] + dot(att[z2], w_buf[w_rows(z2, 0, 256), f])
-        part[n] = last.reshape(4, 32, 512).astype(BF16)
-        for d in (2, 1, 3):
-            y2 = lax.rem(yy + d, 4)
-            remote(part.at[n, y2], got.at[n, yy], send1, recv1.at[yy], y2 * 4 + zz, qblk)
+    wait_bytes(w_buf.at[:, w_rows(zz, 0, 256)], w_sem)
+    for c in range(2):
+        for d in (1, 3, 2):
+            z2 = lax.rem(zz + d, 4)
+            here = w_buf.at[c, w_rows(z2, 128 + core * 64, 64)]
+            wait_bytes(w_buf.at[c, w_rows(z2, 0, 48)], wf_recv.at[c, z2])
+            remote(here, here, w_send, ws_recv.at[c, z2, 1], head, sibling)
+            here = w_buf.at[c, w_rows(z2, core * 64, 64)]
+            wait_bytes(here, wz_recv.at[c, z2])
+            remote(here, here, w_send, ws_recv.at[c, z2, 0], head, sibling)
+        total[...] = dot(att[zz], w_buf[c, w_rows(zz, 0, 256), :])
+        for d in (1, 3, 2):
+            z2 = lax.rem(zz + d, 4)
+            for i in range(2):
+                wait_bytes(w_buf.at[c, w_rows(z2, i * 128 + (1 - core) * 64, 64)], ws_recv.at[c, z2, i])
+            if d != 2:
+                total[...] += dot(att[z2], w_buf[c, w_rows(z2, 0, 256), :])
+        for n in (2 * c, 2 * c + 1):
+            f = slice((n % 2) * 512, (n % 2 + 1) * 512)
+            last = total[:, f] + dot(att[z2], w_buf[c, w_rows(z2, 0, 256), f])
+            part[n] = last.reshape(4, 32, 512).astype(BF16)
+            for d in (2, 1, 3):
+                y2 = lax.rem(yy + d, 4)
+                remote(part.at[n, y2], got.at[n, yy], send1, recv1.at[yy], y2 * 4 + zz, qblk)
 
     for a in range(3):
         wait_bytes(info.at[a, pl.ds(0, 3)], info_recv.at[a])
@@ -383,7 +388,7 @@
         out_ref[:, f] = v.astype(BF16)
     wait_bytes(kv.at[pl.ds(0, 7)], kv_send)
     wait_bytes(q_buf.at[pl.ds(0, 3)], q_send)
-    wait_bytes(w_buf.at[pl.ds(0, 768)], w_send)
+    wait_bytes(w_buf.at[:, pl.ds(0, 768)], w_send)
     wait_bytes(part.at[:, pl.ds(0, 3)], send1)
     wait_bytes(info.at[:, pl.ds(0, 3)], info_send)
     for a in range(3):
@@ -402,21 +407,28 @@
     return pl.pallas_call(
         layer_kernel,
         out_shape=jax.ShapeDtypeStruct((32, D), BF16),
-        in_specs=[hbm, hbm, hbm, vmem, vmem, vmem, vmem, vmem, hbm, hbm, hbm, hbm],
+        in_specs=[hbm, hbm, hbm, hbm, hbm, hbm, hbm, hbm, hbm, hbm, hbm, hbm],
         out_specs=vmem,
         scratch_shapes=[
+            scratch((1, 512), jnp.int32),
+            scratch((32, D), BF16),
+            scratch((1, D), F32),
+            scratch((8, 32), jnp.int32),
+            scratch((8, 32), F32),
+            dma((5,)),
             scratch((8, 2, 256, HD), BF16),
             scratch((4, 4, 32, 2 * HD), BF16),
-            scratch((1024, D), BF16),
+            scratch((4, HD, 256), BF16),
+            scratch((2, 1024, 1024), BF16),
             scratch((HD, 512), BF16),
             scratch((1, 1024), F32),
             scratch((1, 1024), F32),
             scratch((HD, 1024), F32),
             scratch((4, 128, 2 * HD), BF16),
-            scratch((128, D), F32),
+            scratch((128, 1024), F32),
             scratch((4, 4, 32, 512), BF16),
             scratch((4, 4, 32, 512), BF16),
-            dma, dma, dma, dma((8,)), dma, dma((4,)), dma, dma((4,)), dma((4,)), dma((4,)), dma((4, 2)), dma, dma((4,)),
+            dma, dma, dma, dma((8,)), dma, dma((4,)), dma, dma((2, 4)), dma((2, 4)), dma((2, 4)), dma((2, 4, 2)), dma, dma((4,)),
             scratch((D, FF), BF16),
             scratch((D, FF), BF16),
             scratch((FF, D), BF16),

time: 87 us -> 83.4 us (0.959)
  Pallas kernels: 85.2 us -> 81.7 us
    pallas_call x1, Pallas kernels: 85.2 us -> 81.7 us  [per_device(): pl.pallas_call(layer_kernel, out_shape=jax.ShapeDtypeStruct((32, D), BF16...]
where the time goes in v6:
time: 83.4 us; the launch traced here: 83.2 us
  Pallas kernels  81.7 us (98%)
  local copies, waits for them, and re-layouts  1.57 us (2%)
    pallas_call x1, Pallas kernels, per_device(): pl.pallas_call(layer_kernel, out_shape=jax.ShapeDtypeStruct((32, D), BF16...  81.7 us

profile of v6, /device:TPU:1, one launch (start us, length us, event | category | flops | bytes accessed | tf_op | source)
XLA Modules:
  0.0 83.2 jit_solution(9852905590032716427)
XLA Ops:
  0.0 81.7 %layer.1 = bf16[32,2048]{1,0:T(8,128)(2,1)} custom-call(bf16[4,4,32,256]{3,2,1,0:T(8,128)(2,1)} %bitcast.5, bf16[4,256,128]{2,1,0:T(8,128)(2,1)} %key_ref.1, bf16[4,256,128]{2,1,0:T(8,128)(2,1)} %value_ref.1, s32[1,512]{1,0:T(1,128)} %bitcast.9, bf16[32,2048]{1,0:T(8,128)(2,1)} %res_in.1, f32[1,2048]{1,0:T(1,128)} %bitcast.6, s32[8,32]{1,0:T(8,128)} %bitcast.7, ...), custom_call_target="tpu_custom_call" | custom-call | tf_op jit(solution)/shard_map/layer/pallas_call | solution.py:407
  81.7 1.6 %copy.14 = bf16[32,2048]{1,0:T(8,128)(2,1)} copy(bf16[32,2048]{1,0:T(8,128)(2,1)} %layer.1) | data formatting | bytes 262144

commit v7 on v6

--- a/solution.py
+++ b/solution.py
@@ -12,7 +12,7 @@
 FF = 768
 NEG = -1e30
 WIDTH = (640, 640, 768)
-FORWARD = (0, 3)
+FORWARD = {0: (0,), 1: (1,), 3: (2,), 2: (3,)}
 FEATURES = (slice(0, 640), slice(640, 1280), slice(1280, 2048))
 QSCALE = HD ** (-0.5) * 1.4426950408889634
 VMEM_LIMIT = 58 * 1024 * 1024
@@ -188,20 +188,20 @@
         return pl.ds(pl.multiple_of(z * 256 + first, 16), count)
 
     mine16 = 128 + core * 64 + xx * 16
-    half = (slice(0, 1024), slice(1024, 2048))
-    for c in range(2):
+    quarter = [slice(c * 512, (c + 1) * 512) for c in range(4)]
+    for c in range(4):
         for first, count, sems in ((mine16, 16, wx_recv), (core * 64, 64, wz_recv)):
             for d in (1, 3, 2):
                 z2 = lax.rem(zz + d, 4)
-                remote(w_ref.at[w_rows(0, first, count), half[c]], w_buf.at[c, w_rows(zz, first, count)],
+                remote(w_ref.at[w_rows(0, first, count), quarter[c]], w_buf.at[c, w_rows(zz, first, count)],
                        w_send, sems.at[c, zz], yy * 4 + z2, qblk)
     for j, src in enumerate((key_ref, value_ref)):
         pltpu.make_async_copy(src.at[yy], kv.at[qblk, j], own_sem).start()
     pltpu.make_async_copy(q_ref.at[:, zz], q_buf.at[zz], q_recv.at[zz]).start()
     for h, q in y_line:
         signal(plane_sem, h, q)
-    for c in range(2):
-        pltpu.make_async_copy(w_ref.at[:, half[c]], w_buf.at[c, w_rows(zz, 0, 256)], w_sem).start()
+    for c in range(4):
+        pltpu.make_async_copy(w_ref.at[:, quarter[c]], w_buf.at[c, w_rows(zz, 0, 256)], w_sem).start()
     w_copies = [
         pltpu.make_async_copy(src.at[0], dst, e_sem.at[i])
         for i, (src, dst) in enumerate(((wg_ref, wg), (wu_ref, wu), (wd_ref, wd)))
@@ -258,8 +258,7 @@
 
         lax.fori_loop(0, 4, rows, 0, unroll=True)
 
-        if dx in FORWARD:
-            c = FORWARD.index(dx)
+        for c in FORWARD[dx]:
             for d in (1, 3, 2):
                 z2 = lax.rem(zz + d, 4)
                 here = w_buf.at[c, w_rows(z2, mine16, 16)]
@@ -273,7 +272,7 @@
         att[n // 2, :, (n % 2) * HD:(n % 2 + 1) * HD] = (acc[:, cols] / den[:, cols]).T.astype(BF16)
 
     wait_bytes(w_buf.at[:, w_rows(zz, 0, 256)], w_sem)
-    for c in range(2):
+    for c in range(4):
         for d in (1, 3, 2):
             z2 = lax.rem(zz + d, 4)
             here = w_buf.at[c, w_rows(z2, 128 + core * 64, 64)]
@@ -289,13 +288,11 @@
                 wait_bytes(w_buf.at[c, w_rows(z2, i * 128 + (1 - core) * 64, 64)], ws_recv.at[c, z2, i])
             if d != 2:
                 total[...] += dot(att[z2], w_buf[c, w_rows(z2, 0, 256), :])
-        for n in (2 * c, 2 * c + 1):
-            f = slice((n % 2) * 512, (n % 2 + 1) * 512)
-            last = total[:, f] + dot(att[z2], w_buf[c, w_rows(z2, 0, 256), f])
-            part[n] = last.reshape(4, 32, 512).astype(BF16)
-            for d in (2, 1, 3):
-                y2 = lax.rem(yy + d, 4)
-                remote(part.at[n, y2], got.at[n, yy], send1, recv1.at[yy], y2 * 4 + zz, qblk)
+        last = total[...] + dot(att[z2], w_buf[c, w_rows(z2, 0, 256), :])
+        part[c] = last.reshape(4, 32, 512).astype(BF16)
+        for d in (2, 1, 3):
+            y2 = lax.rem(yy + d, 4)
+            remote(part.at[c, y2], got.at[c, yy], send1, recv1.at[yy], y2 * 4 + zz, qblk)
 
     for a in range(3):
         wait_bytes(info.at[a, pl.ds(0, 3)], info_recv.at[a])
@@ -370,13 +367,14 @@
 
     lax.fori_loop(0, 2, one_round, 0)
 
-    for a in range(3):
-        mixed = jnp.zeros((128, WIDTH[a]), F32)
-        for r in range(2):
-            block = slice(r * 256, (r + 1) * 256)
-            wait_bytes(backbox[a].at[block], recv4.at[a, r])
-            mixed += dot(mix[a, 0, :, block], backbox[a][block]) + dot(mix[a, 1, :, block], backbox[a][block])
-        sums[a][...] = mixed.astype(BF16)
+    def mixed(a, r):
+        block = slice(r * 256, (r + 1) * 256)
+        wait_bytes(backbox[a].at[block], recv4.at[a, r])
+        return dot(mix[a, 0, :, block], backbox[a][block]) + dot(mix[a, 1, :, block], backbox[a][block])
+
+    first = [mixed(a, 0) for a in range(3)]
+    for a in range(3):
+        sums[a][...] = (first[a] + mixed(a, 1)).astype(BF16)
         for d, (h, q) in zip((1, 3, 2), peers[a]):
             remote(sums[a].at[rows32(lax.rem(place[a] + d, 4))], others[a].at[rows32(place[a])],
                    sum_send.at[a], sum_recv.at[a], h, q)
@@ -419,16 +417,16 @@
             scratch((8, 2, 256, HD), BF16),
             scratch((4, 4, 32, 2 * HD), BF16),
             scratch((4, HD, 256), BF16),
-            scratch((2, 1024, 1024), BF16),
+            scratch((4, 1024, 512), BF16),
             scratch((HD, 512), BF16),
             scratch((1, 1024), F32),
             scratch((1, 1024), F32),
             scratch((HD, 1024), F32),
             scratch((4, 128, 2 * HD), BF16),
-            scratch((128, 1024), F32),
+            scratch((128, 512), F32),
             scratch((4, 4, 32, 512), BF16),
             scratch((4, 4, 32, 512), BF16),
-            dma, dma, dma, dma((8,)), dma, dma((4,)), dma, dma((2, 4)), dma((2, 4)), dma((2, 4)), dma((2, 4, 2)), dma, dma((4,)),
+            dma, dma, dma, dma((8,)), dma, dma((4,)), dma, dma((4, 4)), dma((4, 4)), dma((4, 4)), dma((4, 4, 2)), dma, dma((4,)),
             scratch((D, FF), BF16),
             scratch((D, FF), BF16),
             scratch((FF, D), BF16),

time: 83.4 us -> 82.5 us (0.989); the launches traced: 83.2 us -> 81.3 us
  Pallas kernels: 81.7 us -> 79.7 us
    pallas_call x1, Pallas kernels: 81.7 us -> 79.7 us  [per_device(): pl.pallas_call(layer_kernel, out_shape=jax.ShapeDtypeStruct((32, D), BF16...]
where the time goes in v7:
time: 82.5 us; the launch traced here: 81.3 us
  Pallas kernels  79.7 us (97%)
  local copies, waits for them, and re-layouts  1.57 us (2%)
    pallas_call x1, Pallas kernels, per_device(): pl.pallas_call(layer_kernel, out_shape=jax.ShapeDtypeStruct((32, D), BF16...  79.7 us

profile of v7, /device:TPU:1, one launch (start us, length us, event | category | flops | bytes accessed | tf_op | source)
XLA Modules:
  0.0 81.3 jit_solution(13134096039843418902)
XLA Ops:
  0.0 79.7 %layer.1 = bf16[32,2048]{1,0:T(8,128)(2,1)} custom-call(bf16[4,4,32,256]{3,2,1,0:T(8,128)(2,1)} %bitcast.5, bf16[4,256,128]{2,1,0:T(8,128)(2,1)} %key_ref.1, bf16[4,256,128]{2,1,0:T(8,128)(2,1)} %value_ref.1, s32[1,512]{1,0:T(1,128)} %bitcast.9, bf16[32,2048]{1,0:T(8,128)(2,1)} %res_in.1, f32[1,2048]{1,0:T(1,128)} %bitcast.6, s32[8,32]{1,0:T(8,128)} %bitcast.7, ...), custom_call_target="tpu_custom_call" | custom-call | tf_op jit(solution)/shard_map/layer/pallas_call | solution.py:405
  79.7 1.6 %copy.14 = bf16[32,2048]{1,0:T(8,128)(2,1)} copy(bf16[32,2048]{1,0:T(8,128)(2,1)} %layer.1) | data formatting | bytes 262144

commit v8 on v7

--- a/solution.py
+++ b/solution.py
@@ -315,22 +315,21 @@
         for h, q in peers[a]:
             remote(here, here, line_send.at[a], line_recv.at[a], h, q)
     pl.semaphore_wait(all_sem, 3)
-    for a in range(3):
-        wait_bytes(lines[a].at[pl.ds(0, 96)], line_recv.at[a])
-
-    def dispatch(m, carry):
-        for a in range(3):
-            h, q = partner(a, head, qblk, m, 1)
-            remote(outbox[a].at[rows16(m)], inbox[a].at[rows16(m)], send3.at[a], recv3.at[a, m // 16], h, q)
-        return carry
-
     for r in range(2):
         block = pl.ds(r * 256, 256)
         for a in range(3):
+            if r == 0:
+                wait_bytes(lines[a].at[pl.ds(0, 96)], line_recv.at[a])
             outbox[a][block] = dot(pick[a, block], lines[a][...]).astype(BF16)
             if r == 0:
                 pltpu.make_async_copy(outbox[a].at[rows16(0)], inbox[a].at[rows16(0)], recv3.at[a, 0]).start()
-        lax.fori_loop(max(r * 16, 1), r * 16 + 16, dispatch, 0)
+
+            def dispatch(m, carry, a=a, r=r):
+                h, q = partner(a, head, qblk, m, 1)
+                remote(outbox[a].at[rows16(m)], inbox[a].at[rows16(m)], send3.at[a], recv3.at[a, r], h, q)
+                return carry
+
+            lax.fori_loop(max(r * 16, 1), r * 16 + 16, dispatch, 0, unroll=True)
 
     for a in range(3):
         sort[a] = one_hot(source(a, head, qblk, iota((256, 256), 1)) == iota((256, 256), 0))

time: 82.5 us -> 81.9 us (level); the launches traced: 81.3 us -> 81.7 us
  no operation moved by 1% of the time
where the time goes in v8:
time: 81.9 us; the launch traced here: 81.7 us
  Pallas kernels  80.2 us (98%)
  local copies, waits for them, and re-layouts  1.57 us (2%)
    pallas_call x1, Pallas kernels, per_device(): pl.pallas_call(layer_kernel, out_shape=jax.ShapeDtypeStruct((32, D), BF16...  80.2 us

profile of v8, /device:TPU:1, one launch (start us, length us, event | category | flops | bytes accessed | tf_op | source)
XLA Modules:
  0.0 81.7 jit_solution(2241547366815259448)
XLA Ops:
  0.0 80.2 %layer.1 = bf16[32,2048]{1,0:T(8,128)(2,1)} custom-call(bf16[4,4,32,256]{3,2,1,0:T(8,128)(2,1)} %bitcast.5, bf16[4,256,128]{2,1,0:T(8,128)(2,1)} %key_ref.1, bf16[4,256,128]{2,1,0:T(8,128)(2,1)} %value_ref.1, s32[1,512]{1,0:T(1,128)} %bitcast.9, bf16[32,2048]{1,0:T(8,128)(2,1)} %res_in.1, f32[1,2048]{1,0:T(1,128)} %bitcast.6, s32[8,32]{1,0:T(8,128)} %bitcast.7, ...), custom_call_target="tpu_custom_call" | custom-call | tf_op jit(solution)/shard_map/layer/pallas_call | solution.py:404
  80.2 1.6 %copy.14 = bf16[32,2048]{1,0:T(8,128)(2,1)} copy(bf16[32,2048]{1,0:T(8,128)(2,1)} %layer.1) | data formatting | bytes 262144

commit v9 on v8

--- a/solution.py
+++ b/solution.py
@@ -361,7 +361,11 @@
             for a in range(3):
                 pltpu.make_async_copy(ybox[a].at[rows16(0)], backbox[a].at[rows16(0)], recv4.at[a, 0]).start()
 
-        lax.fori_loop(jnp.maximum(r * 16, 1), r * 16 + 16, send_back, 0)
+        @pl.when(r != 0)
+        def _():
+            send_back(r * 16, 0)
+
+        lax.fori_loop(0, 15, lambda j, carry: send_back(r * 16 + 1 + j, carry), 0, unroll=True)
         return carry
 
     lax.fori_loop(0, 2, one_round, 0)

time: 81.9 us -> 81.9 us (level)
  no operation moved by 1% of the time
where the time goes in v9:
time: 81.9 us; the launch traced here: 81.8 us
  Pallas kernels  80.2 us (98%)
  local copies, waits for them, and re-layouts  1.57 us (2%)
    pallas_call x1, Pallas kernels, per_device(): pl.pallas_call(layer_kernel, out_shape=jax.ShapeDtypeStruct((32, D), BF16...  80.2 us

profile of v9, /device:TPU:1, one launch (start us, length us, event | category | flops | bytes accessed | tf_op | source)
XLA Modules:
  0.0 81.8 jit_solution(18071161426263642297)
XLA Ops:
  0.0 80.2 %layer.1 = bf16[32,2048]{1,0:T(8,128)(2,1)} custom-call(bf16[4,4,32,256]{3,2,1,0:T(8,128)(2,1)} %bitcast.5, bf16[4,256,128]{2,1,0:T(8,128)(2,1)} %key_ref.1, bf16[4,256,128]{2,1,0:T(8,128)(2,1)} %value_ref.1, s32[1,512]{1,0:T(1,128)} %bitcast.9, bf16[32,2048]{1,0:T(8,128)(2,1)} %res_in.1, f32[1,2048]{1,0:T(1,128)} %bitcast.6, s32[8,32]{1,0:T(8,128)} %bitcast.7, ...), custom_call_target="tpu_custom_call" | custom-call | tf_op jit(solution)/shard_map/layer/pallas_call | solution.py:408
  80.2 1.6 %copy.14 = bf16[32,2048]{1,0:T(8,128)(2,1)} copy(bf16[32,2048]{1,0:T(8,128)(2,1)} %layer.1) | data formatting | bytes 262144
